TPU v7x, 32 devices: a whole 2x2x4 slice. The times are simulated.
32 devices in a mesh: chan: 2 (over y), dp: 16 (over z, x, core).
Axes of the slice: x: 2, y: 2, z: 4, core: 2. Of those that a mesh axis runs over, the one named last changes fastest.
Arguments:
- volume: bfloat16 [32, 32, 32, 256], P('dp', None, None, 'chan'), may hold values from -6 to 6
- filter_one: bfloat16 [3, 3, 3, 256, 256], P(None, None, None, 'chan'), may hold values from -0.078125 to 0.078125
- filter_two: bfloat16 [3, 3, 3, 256, 256], P(None, None, None, 'chan'), may hold values from -0.078125 to 0.078125
- cotangent: bfloat16 [32, 32, 32, 256], P('dp', None, None, 'chan'), may hold values from -6 to 6
Outputs:
- output: bfloat16 [32, 32, 32, 256], P('dp', None, None, 'chan')
- input_grad: bfloat16 [32, 32, 32, 256], P('dp', None, None, 'chan')
- grad_one: float32 [3, 3, 3, 256, 256], P(None, None, None, 'chan')
- grad_two: float32 [3, 3, 3, 256, 256], P(None, None, None, 'chan')
All inputs are finite; a program needn't handle non-finite values.
Results may differ from a plain program's by a relative error of at most 0.02525.
The roundings to bfloat16 on the way count: a program that leaves them out, or rounds other values in their place, can miss the bound.
Values may be sent and summed in bfloat16 or wider, within the bound.
No kernel may reach another device: no remote copies, remote signals or barrier semaphores. Data moves between devices by JAX's collectives and lax.ppermute only.
A program may use at most 128 MiB of HBM per device.

v0:
```python
import functools
import math

import jax
import jax.numpy as jnp
from jax import lax
from jax.experimental import pallas as pl
from jax.experimental.pallas import tpu as pltpu
from jax.sharding import PartitionSpec as P

VOX = 32
SLOPE = 0.3
HALF = 128
FULL = 256
TILE = 16
VMEM_LIMIT = 40 * 1024 * 1024


def extended(block, sides, width):
    for axis, dim in sides:
        count = lax.axis_size(axis)
        forward = [(i, i + 1) for i in range(count - 1)]
        forward.append((count - 1, 0))
        backward = [(target, source) for source, target in forward]
        low = lax.ppermute(
            lax.slice_in_dim(block, block.shape[dim] - width, None, axis=dim), axis, forward
        )
        high = lax.ppermute(lax.slice_in_dim(block, 0, width, axis=dim), axis, backward)
        block = jnp.concatenate([low, block, high], axis=dim)
    return block


def leaky(values):
    return jnp.where(values > 0, values, SLOPE * values)


def slope_of(values):
    return jnp.where(values > 0, jnp.float32(1.0), jnp.float32(SLOPE))


def tap_mask(rows, offset):
    base = lax.axis_index("dp") * rows
    total_rows = lax.axis_size("dp") * rows
    planes = jnp.mod(base + jnp.arange(rows, dtype=jnp.int32) - 1, total_rows)
    depth = jnp.mod(planes, VOX) + offset
    inside = jnp.logical_and(depth >= 0, depth < VOX)
    return inside[:, None, None, None]


def pad_plane(values):
    return jnp.pad(values, ((0, 0), (1, 1), (1, 1), (0, 0)))


def columns(plane, rows, height, breadth):
    taps = []
    for a in range(3):
        inside = tap_mask(rows, a - 1)
        depth_slab = plane[a : a + rows]
        depth_slab = jnp.where(inside, depth_slab, jnp.zeros_like(depth_slab))
        for b in range(3):
            for c in range(3):
                taps.append(depth_slab[:, b : b + height, c : c + breadth, :])
    stacked = jnp.concatenate(taps, axis=-1)
    return stacked.reshape(rows * height * breadth, stacked.shape[-1])


def plain(volume, filter_one, filter_two, cotangent):
    rows, height, breadth, narrow = volume.shape
    full = filter_one.shape[4]
    voxels = rows * height * breadth
    scale = 1.0 / math.sqrt(lax.axis_size("dp") * voxels)

    def forward(activity, weight):
        rim = extended(activity, (("dp", 0),), 1)
        plane = pad_plane(rim)
        stacked = columns(plane, rows, height, breadth)
        partial_value = jnp.dot(
            stacked, weight.reshape(27 * narrow, full), preferred_element_type=jnp.float32
        )
        summed = lax.psum_scatter(partial_value, "chan", scatter_dimension=1, tiled=True)
        return (plane, summed)

    def backward(plane, delta, weight):
        wide = lax.all_gather(delta, "chan", axis=3, tiled=True)
        rim = extended(wide, (("dp", 0),), 1)
        centre = rim[1 : rows + 1].reshape(voxels, full)
        stacked = columns(plane, rows, height, breadth)
        weight_grad = lax.dot_general(
            stacked, centre, (((0,), (0,)), ((), ())), preferred_element_type=jnp.float32
        )
        weight_grad = weight_grad.reshape(3, 3, 3, narrow, full)
        source = pad_plane(rim)
        total = jnp.zeros((rows, height, breadth, narrow), jnp.float32)
        for a in range(3):
            depth_slab = source[2 - a : 2 - a + rows]
            flat = depth_slab.reshape(-1, full)
            product = lax.dot_general(
                flat,
                weight[a].reshape(9 * narrow, full),
                (((1,), (1,)), ((), ())),
                preferred_element_type=jnp.float32,
            )
            product = product.reshape(rows, height + 2, breadth + 2, 9, narrow)
            part = jnp.zeros((rows, height, breadth, narrow), jnp.float32)
            for b in range(3):
                for c in range(3):
                    part = (
                        part
                        + product[:, 2 - b : 2 - b + height, 2 - c : 2 - c + breadth, b * 3 + c, :]
                    )
            inside = tap_mask(rows, 1 - a)
            total = total + jnp.where(inside, part, jnp.zeros_like(part))
        return (weight_grad, total.reshape(voxels, narrow))

    def layer_sum(weight_grad):
        return lax.psum(weight_grad, "dp")

    plane_one, pre_one = forward(volume, filter_one)
    act_one = leaky(pre_one).astype(jnp.bfloat16).reshape(rows, height, breadth, narrow)
    plane_two, pre_two = forward(act_one, filter_two)
    output = leaky(pre_two).astype(jnp.bfloat16).reshape(rows, height, breadth, narrow)
    delta_two = (cotangent.reshape(voxels, narrow).astype(jnp.float32) * slope_of(pre_two)).astype(
        jnp.bfloat16
    )
    local_two, back_two = backward(
        plane_two, delta_two.reshape(rows, height, breadth, narrow), filter_two
    )
    summed_two = layer_sum(local_two)
    delta_one = (back_two * slope_of(pre_one)).astype(jnp.bfloat16)
    local_one, back_one = backward(
        plane_one, delta_one.reshape(rows, height, breadth, narrow), filter_one
    )
    summed_one = layer_sum(local_one)
    input_grad = back_one.astype(jnp.bfloat16).reshape(rows, height, breadth, narrow)
    return (output, input_grad, summed_one * scale, summed_two * scale)


def copy_weights(own_ref, same_ref, swap_ref, full_ref, sems):
    me = lax.axis_index("chan")
    core = lax.rem(lax.axis_index("dp"), 2)
    quarter = HALF // 2
    sources = [(own_ref, HALF, 0)]
    if same_ref is not None:
        sources.append((same_ref, quarter, HALF + core * quarter))
        sources.append((swap_ref, quarter, HALF + (1 - core) * quarter))
    copies = []
    for source, height, row in sources:
        for side in range(2):
            column = pl.multiple_of((me if side == 0 else 1 - me) * HALF, HALF)
            if not isinstance(row, int):
                row = pl.multiple_of(row, quarter)
            copies.append(
                pltpu.make_async_copy(
                    source.at[:, :, pl.ds(column, HALF)],
                    full_ref.at[:, pl.ds(row, height), pl.ds(side * HALF, HALF)],
                    sems.at[len(copies)],
                )
            )
    for copy in copies:
        copy.start()
    return copies


def is_seam():
    return lax.rem(lax.axis_index("dp") * 2, VOX) == 0


def fill_planes(planes, store):
    for slot in range(6):
        store[slot, 0] = jnp.zeros(store.shape[2:], store.dtype)
        store[slot, VOX + 1] = jnp.zeros(store.shape[2:], store.dtype)
    for slot, plane in ((0, 0), (1, 1), (4, 2), (5, 3)):
        for lane, ref, at in planes[plane]:
            store[slot, 1 : VOX + 1, :, lane : lane + ref.shape[3]] = ref[at]
    seam = is_seam()
    for slot, plane in ((2, 2), (3, 1)):

        @pl.when(seam)
        def _():
            store[slot] = jnp.zeros(store.shape[1:], store.dtype)

        @pl.when(jnp.logical_not(seam))
        def _():
            for lane, ref, at in planes[plane]:
                store[slot, 1 : VOX + 1, :, lane : lane + ref.shape[3]] = ref[at]


def conv_rows(store, weights, plane, row, flipped):
    pieces = []
    for a in range(3):
        for b in range(3):
            piece = store[3 * plane + a, pl.ds(row + b, TILE)]
            pieces.append(piece.reshape(TILE * VOX, FULL))
    stacked = jnp.concatenate(pieces, axis=1)
    products = []
    for c in range(3):
        if flipped:
            taps = [weights[(2 - a) * 9 + (2 - b) * 3 + 2 - c] for a in range(3) for b in range(3)]
            dims = (((1,), (1,)), ((), ()))
            taps = jnp.concatenate(taps, axis=1)
        else:
            taps = [weights[a * 9 + b * 3 + c] for a in range(3) for b in range(3)]
            dims = (((1,), (0,)), ((), ()))
            taps = jnp.concatenate(taps, axis=0)
        products.append(
            lax.dot_general(stacked, taps, dims, preferred_element_type=jnp.float32)
        )
    left, middle, right = products
    column = lax.rem(lax.broadcasted_iota(jnp.int32, left.shape, 0), VOX)
    left = jnp.where(column > 0, pltpu.roll(left, 1, 0), 0.0)
    right = jnp.where(column < VOX - 1, pltpu.roll(right, TILE * VOX - 1, 0), 0.0)
    return middle + left + right


def over_tiles(body):
    for plane in range(2):

        @pl.loop(0, VOX // TILE)
        def _(step):
            body(plane, pl.multiple_of(step * TILE, TILE))


def shaped(values):
    return values.reshape(TILE, VOX, values.shape[1])


def first_kernel(
    mid_own, mid_other, low_own, high_own, low_other, high_other, own, same, swap,
    act_0, act_1, weights, store, sems,
):
    copies = copy_weights(own, same, swap, weights, sems)
    fill_planes(
        [
            ((0, low_own, 0), (HALF, low_other, 0)),
            ((0, mid_own, 0), (HALF, mid_other, 0)),
            ((0, mid_own, 1), (HALF, mid_other, 1)),
            ((0, high_own, 0), (HALF, high_other, 0)),
        ],
        store,
    )
    for copy in copies:
        copy.wait()

    def body(plane, row):
        value = leaky(conv_rows(store, weights, plane, row, False))
        target = (act_0, act_1)[plane]
        target[0, pl.ds(row, TILE)] = shaped(value.astype(jnp.bfloat16))

    over_tiles(body)


def second_kernel(
    act_0, act_1, low, high, cot_own, cot_other, own, same, swap,
    output, delta_0, delta_1, weights, store, sems,
):
    copies = copy_weights(own, same, swap, weights, sems)
    fill_planes(
        [((0, low, 0),), ((0, act_0, 0),), ((0, act_1, 0),), ((0, high, 0),)], store
    )
    for copy in copies:
        copy.wait()

    def body(plane, row):
        value = conv_rows(store, weights, plane, row, False)
        output[plane, pl.ds(row, TILE)] = shaped(leaky(value[:, :HALF]).astype(jnp.bfloat16))
        slope = slope_of(value)
        target = (delta_0, delta_1)[plane]
        for lane, cot in ((0, cot_own), (HALF, cot_other)):
            grad = cot[plane, pl.ds(row, TILE)].astype(jnp.float32)
            delta = grad * shaped(slope[:, lane : lane + HALF])
            target[0, pl.ds(row, TILE), :, lane : lane + HALF] = delta.astype(jnp.bfloat16)

    over_tiles(body)


def back_kernel(
    delta_0, delta_1, low, high, act_0, act_1, own, same, swap,
    prior_0, prior_1, weights, store, sems,
):
    copies = copy_weights(own, same, swap, weights, sems)
    fill_planes(
        [((0, low, 0),), ((0, delta_0, 0),), ((0, delta_1, 0),), ((0, high, 0),)], store
    )
    for copy in copies:
        copy.wait()

    def body(plane, row):
        value = shaped(conv_rows(store, weights, plane, row, True))
        act = (act_0, act_1)[plane][0, pl.ds(row, TILE)].astype(jnp.float32)
        target = (prior_0, prior_1)[plane]
        target[0, pl.ds(row, TILE)] = (value * slope_of(act)).astype(jnp.bfloat16)

    over_tiles(body)


def last_kernel(delta_0, delta_1, low, high, own, grad, weights, store, sems):
    copies = copy_weights(own, None, None, weights, sems)
    fill_planes(
        [((0, low, 0),), ((0, delta_0, 0),), ((0, delta_1, 0),), ((0, high, 0),)], store
    )
    for copy in copies:
        copy.wait()

    def body(plane, row):
        value = conv_rows(store, weights, plane, row, True)
        grad[plane, pl.ds(row, TILE)] = shaped(value.astype(jnp.bfloat16))

    over_tiles(body)


def filter_kernel(low, mid_0, mid_1, high, delta_0, delta_1, keep, send, turned, moved):
    pixels = VOX * VOX
    seam = is_seam()
    sources = ((0, low), (1, mid_0), (2, mid_1), (3, high))
    for plane, ref in sources:
        flipped = ref[0].reshape(pixels, HALF).T
        for output_plane in range(2):
            tap = plane - output_plane
            if not 0 <= tap < 3:
                continue
            rows = slice(tap * HALF, (tap + 1) * HALF)
            columns = slice(output_plane * pixels, (output_plane + 1) * pixels)
            if plane in (1, 2) and tap != 1:
                turned[rows, columns] = jnp.where(seam, jnp.zeros_like(flipped), flipped)
            else:
                turned[rows, columns] = flipped
    for plane, ref in ((0, delta_0), (1, delta_1)):
        for c in range(3):
            moved[c, plane, 0] = jnp.zeros(moved.shape[3:], moved.dtype)
            moved[c, plane, VOX + 1] = jnp.zeros(moved.shape[3:], moved.dtype)
        moved[1, plane, 1 : VOX + 1] = ref[0]

        @pl.loop(0, VOX // TILE)
        def _(step):
            row = step * TILE
            values = ref[0, pl.ds(row, TILE)].reshape(TILE * VOX, FULL).astype(jnp.float32)
            column = lax.rem(lax.broadcasted_iota(jnp.int32, values.shape, 0), VOX)
            ahead = jnp.where(column < VOX - 1, pltpu.roll(values, TILE * VOX - 1, 0), 0.0)
            behind = jnp.where(column > 0, pltpu.roll(values, 1, 0), 0.0)
            moved[0, plane, pl.ds(row + 1, TILE)] = shaped(ahead.astype(jnp.bfloat16))
            moved[2, plane, pl.ds(row + 1, TILE)] = shaped(behind.astype(jnp.bfloat16))

    mine = lax.axis_index("chan") == lax.rem(lax.axis_index("dp"), 2)
    for b in range(3):

        @pl.loop(0, 3)
        def _(c):
            right = moved[c, :, 2 - b : 2 - b + VOX].reshape(2 * pixels, FULL)
            product = jnp.dot(turned[...], right, preferred_element_type=jnp.float32)
            kept = jnp.where(mine, product[:, :HALF], product[:, HALF:])
            sent = jnp.where(mine, product[:, HALF:], product[:, :HALF])
            for a in range(3):
                rows = slice(a * HALF, (a + 1) * HALF)
                tap = a * 9 + b * 3 + c
                keep[:, tap] = kept[rows].reshape(8, 16, HALF)
                send[:, tap] = sent[rows].reshape(8, 16, HALF).astype(send.dtype)


def place():
    at = lax.axis_index("dp")
    return at // 4, lax.rem(at // 2, 2), lax.rem(at, 2)


def add_core_kernel(keep, came, kept, sent):
    _, side, _ = place()
    for target, first in ((kept, side * 4), (sent, (1 - side) * 4)):

        @pl.loop(0, 4)
        def _(block):
            total = keep[first + block] + came[first + block].astype(jnp.float32)
            target[block] = total.astype(target.dtype)


def add_side_kernel(keep, came, kept, *sent):
    level, _, _ = place()
    for step, target in enumerate((kept,) + sent):
        block = lax.rem(level + step, 4)
        total = keep[block] + came[block].astype(jnp.float32)
        target[...] = total.astype(target.dtype)


def add_level_kernel(scale, keep, *rest):
    total = keep[...]
    for came in rest[:-1]:
        total = total + came[...].astype(jnp.float32)
    rest[-1][...] = (total * scale).astype(rest[-1].dtype)


def join_level_kernel(own, *rest):
    level, _, _ = place()
    target = rest[-1]
    target[level] = own[...]
    for step, came in enumerate(rest[:-1], 1):
        target[lax.rem(level + 4 - step, 4)] = came[...]


def join_side_kernel(own, came, target):
    _, side, _ = place()
    target[pl.ds(side * 4, 4)] = own[...]
    target[pl.ds((1 - side) * 4, 4)] = came[...]


def join_core_kernel(own, came, grad):
    _, _, core = place()

    @pl.loop(0, 8)
    def _(block):
        row = pl.multiple_of(block * 16, 16)
        first = jnp.where(core == 0, own[block], came[block])
        second = jnp.where(core == 0, came[block], own[block])
        grad[:, pl.ds(row, 16), :HALF] = first.astype(jnp.float32)
        grad[:, pl.ds(row, 16), HALF:] = second.astype(jnp.float32)


def small_call(kernel, outs, operands, name):
    moved = sum(ref.size * ref.dtype.itemsize for ref in operands)
    moved += sum(math.prod(shape) * jnp.dtype(dtype).itemsize for shape, dtype in outs)
    return pl.pallas_call(
        kernel,
        out_shape=[jax.ShapeDtypeStruct(shape, dtype) for shape, dtype in outs],
        in_specs=[pl.BlockSpec(memory_space=pltpu.VMEM)] * len(operands),
        out_specs=[pl.BlockSpec(memory_space=pltpu.VMEM)] * len(outs),
        compiler_params=pltpu.CompilerParams(vmem_limit_bytes=VMEM_LIMIT),
        cost_estimate=pl.CostEstimate(flops=0, bytes_accessed=moved, transcendentals=0),
        name=name,
    )(*operands)


def layer_sum(keep, send, scale, name):
    count = lax.axis_size("dp")
    wide, thin = jnp.float32, jnp.bfloat16
    cores = [(i, i ^ 1) for i in range(count)]
    sides = [(i, i ^ 2) for i in range(count)]
    levels = [[(i, (i + 4 * step) % count) for i in range(count)] for step in (1, 2, 3)]
    part = (27, 16, HALF)

    came = lax.ppermute(send, "dp", cores)
    keep, send = small_call(
        add_core_kernel, [((4,) + part, wide), ((4,) + part, thin)], [keep, came], name + "_core"
    )
    came = lax.ppermute(send, "dp", sides)
    keep, *sends = small_call(
        add_side_kernel, [(part, wide)] + [(part, thin)] * 3, [keep, came], name + "_side"
    )
    came = [lax.ppermute(block, "dp", pairs) for block, pairs in zip(sends, levels)]
    (own,) = small_call(
        functools.partial(add_level_kernel, scale), [(part, thin)], [keep, *came], name + "_level"
    )
    came = [lax.ppermute(own, "dp", pairs) for pairs in levels]
    (own,) = small_call(join_level_kernel, [((4,) + part, thin)], [own, *came], name + "_levels")
    came = lax.ppermute(own, "dp", sides)
    (own,) = small_call(join_side_kernel, [((8,) + part, thin)], [own, came], name + "_sides")
    came = lax.ppermute(own, "dp", cores)
    (grad,) = small_call(join_core_kernel, [((27, HALF, FULL), wide)], [own, came], name + "_cores")
    return grad


def conv_call(kernel, outs, operands, weight_rows, name):
    flops = 2 * 2 * VOX * VOX * 27 * FULL * weight_rows
    count = sum(ref.size * 2 for ref in operands)
    narrow = weight_rows == HALF
    specs = [pl.BlockSpec(memory_space=pltpu.VMEM)] * (len(operands) - (1 if narrow else 3))
    specs += [pl.BlockSpec(memory_space=pl.ANY)] * (1 if narrow else 3)
    return pl.pallas_call(
        kernel,
        out_shape=[jax.ShapeDtypeStruct(shape, jnp.bfloat16) for shape in outs],
        in_specs=specs,
        out_specs=[pl.BlockSpec(memory_space=pltpu.VMEM)] * len(outs),
        scratch_shapes=[
            pltpu.VMEM((27, weight_rows, FULL), jnp.bfloat16),
            pltpu.VMEM((6, VOX + 2, VOX, FULL), jnp.bfloat16),
            pltpu.SemaphoreType.DMA((6,)),
        ],
        compiler_params=pltpu.CompilerParams(vmem_limit_bytes=VMEM_LIMIT),
        cost_estimate=pl.CostEstimate(flops=flops, bytes_accessed=count, transcendentals=0),
        name=name,
    )(*operands)


def filter_call(planes, mid_at, deltas, name):
    narrow = (1, VOX, VOX, HALF)
    specs = [
        pl.BlockSpec(narrow, functools.partial(lambda at, i: (at, 0, 0, 0), at)) for at in mid_at
    ]
    specs += [pl.BlockSpec((1, VOX, VOX, FULL), lambda i: (0, 0, 0, 0))] * 2
    return pl.pallas_call(
        filter_kernel,
        grid=(1,),
        out_shape=[
            jax.ShapeDtypeStruct((8, 27, 16, HALF), jnp.float32),
            jax.ShapeDtypeStruct((8, 27, 16, HALF), jnp.bfloat16),
        ],
        in_specs=specs,
        out_specs=[pl.BlockSpec((8, 27, 16, HALF), lambda i: (0, 0, 0, 0))] * 2,
        scratch_shapes=[
            pltpu.VMEM((3 * HALF, 2 * VOX * VOX), jnp.bfloat16),
            pltpu.VMEM((3, 2, VOX + 2, VOX, FULL), jnp.bfloat16),
        ],
        compiler_params=pltpu.CompilerParams(vmem_limit_bytes=VMEM_LIMIT),
        cost_estimate=pl.CostEstimate(
            flops=2 * 2 * VOX * VOX * 27 * HALF * FULL, bytes_accessed=8 << 20, transcendentals=0
        ),
        name=name,
    )(*planes, *deltas)


def after(value, *earlier):
    return lax.optimization_barrier((value,) + earlier)[0]


def paired(volume, filter_one, filter_two, cotangent):
    count = lax.axis_size("dp")
    ahead = [(i, (i + 1) % count) for i in range(count)]
    behind = [(target, source) for source, target in ahead]
    cores = [(i, i ^ 1) for i in range(count)]
    across = [(0, 1), (1, 0)]
    core = lax.rem(lax.axis_index("dp"), 2)
    scale = 1.0 / math.sqrt(count * 2 * VOX * VOX)
    one = filter_one.reshape(27, HALF, FULL)
    two = filter_two.reshape(27, HALF, FULL)

    def other(values):
        return lax.ppermute(values, "chan", across)

    def rims(first, last):
        return lax.ppermute(last, "dp", ahead), lax.ppermute(first, "dp", behind)

    def my_part(weight):
        return lax.dynamic_slice_in_dim(weight, core * (HALF // 2), HALF // 2, axis=1)

    volume_other = other(volume)
    low_own, high_own = rims(volume[:1], volume[1:])
    one_same = other(my_part(one))
    low_other, high_other = rims(volume_other[:1], volume_other[1:])
    one_swap = lax.ppermute(one_same, "dp", cores)
    two_same = other(after(my_part(two), one_same))
    cot_other = other(after(cotangent, one_same))
    wide = (1, VOX, VOX, FULL)
    narrow = (2, VOX, VOX, HALF)
    act_0, act_1 = conv_call(
        first_kernel,
        [wide, wide],
        [volume, volume_other, low_own, high_own, low_other, high_other, one, one_same, one_swap],
        FULL,
        "first_layer",
    )
    low_act, high_act = rims(act_0, act_1)
    two_swap = lax.ppermute(after(two_same, act_0), "dp", cores)
    output, delta_0, delta_1 = conv_call(
        second_kernel,
        [narrow, wide, wide],
        [act_0, act_1, low_act, high_act, cotangent, cot_other, two, two_same, two_swap],
        FULL,
        "second_layer",
    )
    low_delta, high_delta = rims(delta_0, delta_1)
    local_two = filter_call(
        [low_act, act_0, act_1, high_act], (0, 0, 0, 0), [delta_0, delta_1], "grad_two"
    )
    summed_two = layer_sum(*local_two, scale, "sum_two")
    prior_0, prior_1 = conv_call(
        back_kernel,
        [wide, wide],
        [delta_0, delta_1, low_delta, high_delta, act_0, act_1, two, two_same, two_swap],
        FULL,
        "second_back",
    )
    low_prior, high_prior = rims(prior_0, prior_1)
    local_one = filter_call(
        [low_own, volume, volume, high_own], (0, 0, 1, 0), [prior_0, prior_1], "grad_one"
    )
    summed_one = layer_sum(*local_one, scale, "sum_one")
    (input_grad,) = conv_call(
        last_kernel, [narrow], [prior_0, prior_1, low_prior, high_prior, one], HALF, "first_back"
    )
    shape = filter_one.shape
    return (
        output,
        input_grad,
        summed_one.reshape(shape),
        summed_two.reshape(shape),
    )


def local(volume, filter_one, filter_two, cotangent):
    pair = lax.axis_size("chan") == 2 and lax.axis_size("dp") == 16
    if pair and volume.shape == (2, VOX, VOX, HALF):
        return paired(volume, filter_one, filter_two, cotangent)
    return plain(volume, filter_one, filter_two, cotangent)


def solution(mesh):
    in_specs = (
        P("dp", None, None, "chan"),
        P(None, None, None, "chan", None),
        P(None, None, None, "chan", None),
        P("dp", None, None, "chan"),
    )
    out_specs = (
        P("dp", None, None, "chan"),
        P("dp", None, None, "chan"),
        P(None, None, None, "chan", None),
        P(None, None, None, "chan", None),
    )
    return jax.shard_map(local, mesh=mesh, in_specs=in_specs, out_specs=out_specs, check_vma=False)
```

profile of v0, /device:TPU:0, one launch (start us, length us, event | category | flops | bytes accessed | tf_op | source)
XLA Modules:
  0.0 213.0 jit_solution(2744832209522299738)
XLA Ops:
  5.2 20.4 %collective-permute-done.5.same = bf16[27,64,256]{2,1,0:T(8,128)(2,1)S(1)} collective-permute-done((bf16[27,64,256]{2,1,0:T(8,128)(2,1)S(1)}, bf16[27,64,256]{2,1,0:T(8,128)(2,1)S(1)}, u32[]{:S(2)}, u32[]{:S(2)}) %collective-permute-start.5) | collective-permute-done | bytes 884768 | tf_op jit(solution)/shard_map/ppermute | solution.py:523
  25.6 5.2 %collective-permute-start.2 = (bf16[1,32,32,128]{3,2,1,0:T(8,128)(2,1)S(1)}, bf16[1,32,32,128]{3,2,1,0:T(8,128)(2,1)S(1)}, u32[]{:S(2)}, u32[]{:S(2)}) collective-permute-start(bf16[1,32,32,128]{3,2,1,0:T(8,128)(2,1)S(1)} %get-tuple-element.58), channel_id=1, source_target_pairs={{1,0},{2,1},{3,2},{4,3},{5,4},{6,5},{7,6},{8,7},{9,8},{10,9},{11,1... | collective-permute-start | bytes 786440 | tf_op jit(solution)/shard_map/ppermute | solution.py:526
  30.9 5.1 %collective-permute-done.mid_other = bf16[2,32,32,128]{3,2,1,0:T(8,128)(2,1)S(1)} collective-permute-done((bf16[2,32,32,128]{3,2,1,0:T(8,128)(2,1)S(1)}, bf16[2,32,32,128]{3,2,1,0:T(8,128)(2,1)S(1)}, u32[]{:S(2)}, u32[]{:S(2)}) %collective-permute-start) | collective-permute-done | bytes 524320 | tf_op jit(solution)/shard_map/ppermute | solution.py:523
  36.0 3.4 %collective-permute-start.4 = (bf16[1,32,32,128]{3,2,1,0:T(8,128)(2,1)S(1)}, bf16[1,32,32,128]{3,2,1,0:T(8,128)(2,1)S(1)}, u32[]{:S(2)}, u32[]{:S(2)}) collective-permute-start(bf16[1,32,32,128]{3,2,1,0:T(8,128)(2,1)S(1)} %get-tuple-element.56), channel_id=1, source_target_pairs={{1,0},{2,1},{3,2},{4,3},{5,4},{6,5},{7,6},{8,7},{9,8},{10,9},{11,1... | collective-permute-start | bytes 786440 | tf_op jit(solution)/shard_map/ppermute | solution.py:526
  43.3 4.6 %collective-permute-done.3.low_other = bf16[1,32,32,128]{3,2,1,0:T(8,128)(2,1)S(1)} collective-permute-done((bf16[1,32,32,128]{3,2,1,0:T(8,128)(2,1)S(1)}, bf16[1,32,32,128]{3,2,1,0:T(8,128)(2,1)S(1)}, u32[]{:S(2)}, u32[]{:S(2)}) %collective-permute-start.3) | collective-permute-done | bytes 262176 | tf_op jit(solution)/shard_map/ppermute | solution.py:526
  47.9 9.1 %first_layer.1 = (bf16[1,32,32,256]{3,2,1,0:T(8,128)(2,1)S(1)}, bf16[1,32,32,256]{3,2,1,0:T(8,128)(2,1)S(1)}) custom-call(bf16[2,32,32,128]{3,2,1,0:T(8,128)(2,1)S(1)} %copy-done, bf16[2,32,32,128]{3,2,1,0:T(8,128)(2,1)S(1)} %collective-permute-done.mid_other, bf16[1,32,32,128]{3,2,1,0:T(8,128)(2,1)S(1)} %collective-permute-done.1.low_own.low, ...), custom_call_target="tpu_custom_call" | custom-call | flops 7247757312 | bytes 5636096 | tf_op jit(solution)/shard_map/first_layer/pallas_call | solution.py:464
  61.5 4.2 %collective-permute-start.8 = (bf16[1,32,32,256]{3,2,1,0:T(8,128)(2,1)S(1)}, bf16[1,32,32,256]{3,2,1,0:T(8,128)(2,1)S(1)}, u32[]{:S(2)}, u32[]{:S(2)}) collective-permute-start(bf16[1,32,32,256]{3,2,1,0:T(8,128)(2,1)S(1)} %get-tuple-element.30.act_0.mid_0), channel_id=1, source_target_pairs={{1,0},{2,1},{3,2},{4,3},{5,4},{6,5},{7,6},{8,7},{9,8},{10,9},{11,1... | collective-permute-start | bytes 1572872 | tf_op jit(solution)/shard_map/ppermute | solution.py:526
  65.7 8.4 %collective-permute-done.9.cot_other = bf16[2,32,32,128]{3,2,1,0:T(8,128)(2,1)S(1)} collective-permute-done((bf16[2,32,32,128]{3,2,1,0:T(8,128)(2,1)S(1)}, bf16[2,32,32,128]{3,2,1,0:T(8,128)(2,1)S(1)}, u32[]{:S(2)}, u32[]{:S(2)}) %collective-permute-start.9) | collective-permute-done | bytes 524320 | tf_op jit(solution)/shard_map/ppermute | solution.py:523
  74.1 9.9 %second_layer.1 = (bf16[2,32,32,128]{3,2,1,0:T(8,128)(2,1)}, bf16[1,32,32,256]{3,2,1,0:T(8,128)(2,1)S(1)}, bf16[1,32,32,256]{3,2,1,0:T(8,128)(2,1)S(1)}) custom-call(bf16[1,32,32,256]{3,2,1,0:T(8,128)(2,1)S(1)} %get-tuple-element.30.act_0.mid_0, bf16[1,32,32,256]{3,2,1,0:T(8,128)(2,1)S(1)} %get-tuple-element.31.act_1.mid_1, ...), custom_call_target="tpu_custom_call" | custom-call | flops 7247757312 | bytes 6684672 | tf_op jit(solution)/shard_map/second_layer/pallas_call | solution.py:464
  87.0 6.2 %grad_two.1 = (f32[8,27,16,128]{3,2,1,0:T(8,128)S(1)}, bf16[8,27,16,128]{3,2,1,0:T(8,128)(2,1)S(1)}) custom-call(bf16[1,32,32,256]{3,2,1,0:T(8,128)(2,1)S(1)} %collective-permute-done.7.low, bf16[1,32,32,256]{3,2,1,0:T(8,128)(2,1)S(1)} %get-tuple-element.30.act_0.mid_0, bf16[1,32,32,256]{3,2,1,0:T(8,128)(2,1)S(1)} %get-tuple-element.31.act_1.mid_1, ...), custom_call_target="tpu_custom_call" | custom-call | flops 3623878656 | bytes 8388608 | tf_op jit(solution)/shard_map/grad_two/pallas_call | solution.py:486
  94.7 3.7 %collective-permute-done.12.low = bf16[1,32,32,256]{3,2,1,0:T(8,128)(2,1)S(1)} collective-permute-done((bf16[1,32,32,256]{3,2,1,0:T(8,128)(2,1)S(1)}, bf16[1,32,32,256]{3,2,1,0:T(8,128)(2,1)S(1)}, u32[]{:S(2)}, u32[]{:S(2)}) %collective-permute-start.12) | collective-permute-done | bytes 524320 | tf_op jit(solution)/shard_map/ppermute | solution.py:526
  98.4 9.0 %second_back.1 = (bf16[1,32,32,256]{3,2,1,0:T(8,128)(2,1)S(1)}, bf16[1,32,32,256]{3,2,1,0:T(8,128)(2,1)S(1)}) custom-call(bf16[1,32,32,256]{3,2,1,0:T(8,128)(2,1)S(1)} %get-tuple-element.36.delta_0, bf16[1,32,32,256]{3,2,1,0:T(8,128)(2,1)S(1)} %get-tuple-element.37.delta_1, bf16[1,32,32,256]{3,2,1,0:T(8,128)(2,1)S(1)} %collective-permute-done.12.low, ...), custom_call_target="tpu_custom_call" | custom-call | flops 7247757312 | bytes 6684672 | tf_op jit(solution)/shard_map/second_back/pallas_call | solution.py:464
  107.5 6.1 %grad_one.1 = (f32[8,27,16,128]{3,2,1,0:T(8,128)S(1)}, bf16[8,27,16,128]{3,2,1,0:T(8,128)(2,1)S(1)}) custom-call(bf16[1,32,32,128]{3,2,1,0:T(8,128)(2,1)S(1)} %collective-permute-done.1.low_own.low, bf16[2,32,32,128]{3,2,1,0:T(8,128)(2,1)S(1)} %copy-done, bf16[2,32,32,128]{3,2,1,0:T(8,128)(2,1)S(1)} %copy-done, ...), custom_call_target="tpu_custom_call" | custom-call | flops 3623878656 | bytes 8388608 | tf_op jit(solution)/shard_map/grad_one/pallas_call | solution.py:486
  118.8 10.7 %collective-permute-done.27.came = bf16[4,27,16,128]{3,2,1,0:T(8,128)(2,1)S(1)} collective-permute-done((bf16[4,27,16,128]{3,2,1,0:T(8,128)(2,1)S(1)}, bf16[4,27,16,128]{3,2,1,0:T(8,128)(2,1)S(1)}, u32[]{:S(2)}, u32[]{:S(2)}) %collective-permute-start.27) | collective-permute-done | bytes 442400 | tf_op jit(solution)/shard_map/ppermute | solution.py:441
  133.5 4.6 %collective-permute-done.17.came = bf16[4,27,16,128]{3,2,1,0:T(8,128)(2,1)S(1)} collective-permute-done((bf16[4,27,16,128]{3,2,1,0:T(8,128)(2,1)S(1)}, bf16[4,27,16,128]{3,2,1,0:T(8,128)(2,1)S(1)}, u32[]{:S(2)}, u32[]{:S(2)}) %collective-permute-start.17) | collective-permute-done | bytes 442400 | tf_op jit(solution)/shard_map/ppermute | solution.py:441
  138.2 3.4 %collective-permute-start.19 = (bf16[27,16,128]{2,1,0:T(8,128)(2,1)S(1)}, bf16[27,16,128]{2,1,0:T(8,128)(2,1)S(1)}, u32[]{:S(2)}, u32[]{:S(2)}) collective-permute-start(bf16[27,16,128]{2,1,0:T(8,128)(2,1)S(1)} %get-tuple-element.46), channel_id=1, source_target_pairs={{0,8},{1,9},{2,10},{3,11},{4,12},{5,13},{6,14},{7,15},{8,0},{9,1},... | collective-permute-start | bytes 331784 | tf_op jit(solution)/shard_map/ppermute | solution.py:445
  146.0 5.8 %collective-permute-start.31 = (bf16[27,16,128]{2,1,0:T(8,128)(2,1)S(1)}, bf16[27,16,128]{2,1,0:T(8,128)(2,1)S(1)}, u32[]{:S(2)}, u32[]{:S(2)}) collective-permute-start(bf16[27,16,128]{2,1,0:T(8,128)(2,1)S(1)} %sum_two_level.1.own), channel_id=1, source_target_pairs={{0,4},{1,5},{2,6},{3,7},{4,8},{5,9},{6,10},{7,11},{8,12},{9,13},{1... | collective-permute-start | bytes 331784 | tf_op jit(solution)/shard_map/ppermute | solution.py:449
  152.0 6.5 %collective-permute-start.23 = (bf16[27,16,128]{2,1,0:T(8,128)(2,1)S(1)}, bf16[27,16,128]{2,1,0:T(8,128)(2,1)S(1)}, u32[]{:S(2)}, u32[]{:S(2)}) collective-permute-start(bf16[27,16,128]{2,1,0:T(8,128)(2,1)S(1)} %sum_one_level.1.own), channel_id=1, source_target_pairs={{0,12},{1,13},{2,14},{3,15},{4,0},{5,1},{6,2},{7,3},{8,4},{9,5},{1... | collective-permute-start | bytes 331784 | tf_op jit(solution)/shard_map/ppermute | solution.py:449
  159.1 6.5 %collective-permute-done.32.rest_1_ = bf16[27,16,128]{2,1,0:T(8,128)(2,1)S(1)} collective-permute-done((bf16[27,16,128]{2,1,0:T(8,128)(2,1)S(1)}, bf16[27,16,128]{2,1,0:T(8,128)(2,1)S(1)}, u32[]{:S(2)}, u32[]{:S(2)}) %collective-permute-start.32) | collective-permute-done | bytes 110624 | tf_op jit(solution)/shard_map/ppermute | solution.py:449
  171.9 6.9 %collective-permute-done.34.came = bf16[4,27,16,128]{3,2,1,0:T(8,128)(2,1)S(1)} collective-permute-done((bf16[4,27,16,128]{3,2,1,0:T(8,128)(2,1)S(1)}, bf16[4,27,16,128]{3,2,1,0:T(8,128)(2,1)S(1)}, u32[]{:S(2)}, u32[]{:S(2)}) %collective-permute-start.34) | collective-permute-done | bytes 442400 | tf_op jit(solution)/shard_map/ppermute | solution.py:451
  179.0 8.5 %collective-permute-done.24.came = bf16[4,27,16,128]{3,2,1,0:T(8,128)(2,1)S(1)} collective-permute-done((bf16[4,27,16,128]{3,2,1,0:T(8,128)(2,1)S(1)}, bf16[4,27,16,128]{3,2,1,0:T(8,128)(2,1)S(1)}, u32[]{:S(2)}, u32[]{:S(2)}) %collective-permute-start.24) | collective-permute-done | bytes 442400 | tf_op jit(solution)/shard_map/ppermute | solution.py:451
  188.1 6.2 %collective-permute-done.15.high = bf16[1,32,32,256]{3,2,1,0:T(8,128)(2,1)S(1)} collective-permute-done((bf16[1,32,32,256]{3,2,1,0:T(8,128)(2,1)S(1)}, bf16[1,32,32,256]{3,2,1,0:T(8,128)(2,1)S(1)}, u32[]{:S(2)}, u32[]{:S(2)}) %collective-permute-start.15) | collective-permute-done | bytes 524320 | tf_op jit(solution)/shard_map/ppermute | solution.py:526
  194.3 4.8 %collective-permute-done.14.low = bf16[1,32,32,256]{3,2,1,0:T(8,128)(2,1)S(1)} collective-permute-done((bf16[1,32,32,256]{3,2,1,0:T(8,128)(2,1)S(1)}, bf16[1,32,32,256]{3,2,1,0:T(8,128)(2,1)S(1)}, u32[]{:S(2)}, u32[]{:S(2)}) %collective-permute-start.14) | collective-permute-done | bytes 524320 | tf_op jit(solution)/shard_map/ppermute | solution.py:526
  199.1 9.6 %first_back.1 = bf16[2,32,32,128]{3,2,1,0:T(8,128)(2,1)} custom-call(bf16[1,32,32,256]{3,2,1,0:T(8,128)(2,1)S(1)} %get-tuple-element.38.delta_0, bf16[1,32,32,256]{3,2,1,0:T(8,128)(2,1)S(1)} %get-tuple-element.39.delta_1, bf16[1,32,32,256]{3,2,1,0:T(8,128)(2,1)S(1)} %collective-permute-done.14.low, ...), custom_call_target="tpu_custom_call" | custom-call | flops 3623878656 | bytes 3866624 | tf_op jit(solution)/shard_map/first_back/pallas_call | solution.py:464
  (78 shorter events, 43.2 us)
Async XLA Ops:
  2.1 23.5 %collective-permute-start.5 = (bf16[27,64,256]{2,1,0:T(8,128)(2,1)S(1)}, bf16[27,64,256]{2,1,0:T(8,128)(2,1)S(1)}, u32[]{:S(2)}, u32[]{:S(2)}) collective-permute-start(bf16[27,64,256]{2,1,0:T(8,128)(2,1)S(1)} %constant_dynamic-slice_fusion.1), channel_id=1, source_target_pairs={{0,16},{16,0},{1,17},{17,1},{2,18},{18,2},{3,19},{19,3},{4,20},{20... | collective-permute-start | bytes 2654216 | tf_op jit(solution)/shard_map/ppermute | solution.py:523
  5.1 30.9 %collective-permute-start = (bf16[2,32,32,128]{3,2,1,0:T(8,128)(2,1)S(1)}, bf16[2,32,32,128]{3,2,1,0:T(8,128)(2,1)S(1)}, u32[]{:S(2)}, u32[]{:S(2)}) collective-permute-start(bf16[2,32,32,128]{3,2,1,0:T(8,128)(2,1)S(1)} %copy-done), channel_id=1, source_target_pairs={{0,16},{16,0},{1,17},{17,1},{2,18},{18,2},{3,19},{19,3},{4,20},{20... | collective-permute-start | bytes 1572872 | tf_op jit(solution)/shard_map/ppermute | solution.py:523
  25.6 22.3 %collective-permute-start.6 = (bf16[27,64,256]{2,1,0:T(8,128)(2,1)S(1)}, bf16[27,64,256]{2,1,0:T(8,128)(2,1)S(1)}, u32[]{:S(2)}, u32[]{:S(2)}) collective-permute-start(bf16[27,64,256]{2,1,0:T(8,128)(2,1)S(1)} %collective-permute-done.5.same), channel_id=1, source_target_pairs={{0,1},{1,0},{2,3},{3,2},{4,5},{5,4},{6,7},{7,6},{8,9},{9,8},{10,11... | collective-permute-start | bytes 2654216 | tf_op jit(solution)/shard_map/ppermute | solution.py:535
  25.6 13.9 %collective-permute-start.2 = (bf16[1,32,32,128]{3,2,1,0:T(8,128)(2,1)S(1)}, bf16[1,32,32,128]{3,2,1,0:T(8,128)(2,1)S(1)}, u32[]{:S(2)}, u32[]{:S(2)}) collective-permute-start(bf16[1,32,32,128]{3,2,1,0:T(8,128)(2,1)S(1)} %get-tuple-element.58), channel_id=1, source_target_pairs={{1,0},{2,1},{3,2},{4,3},{5,4},{6,5},{7,6},{8,7},{9,8},{10,9},{11,1... | collective-permute-start | bytes 786440 | tf_op jit(solution)/shard_map/ppermute | solution.py:526
  39.5 20.2 %collective-permute-start.10 = (bf16[27,64,256]{2,1,0:T(8,128)(2,1)S(1)}, bf16[27,64,256]{2,1,0:T(8,128)(2,1)S(1)}, u32[]{:S(2)}, u32[]{:S(2)}) collective-permute-start(bf16[27,64,256]{2,1,0:T(8,128)(2,1)S(1)} %constant_dynamic-slice_fusion), channel_id=1, source_target_pairs={{0,16},{16,0},{1,17},{17,1},{2,18},{18,2},{3,19},{19,3},{4,20},{20... | collective-permute-start | bytes 2654216 | tf_op jit(solution)/shard_map/ppermute | solution.py:523
  59.7 14.4 %collective-permute-start.11 = (bf16[27,64,256]{2,1,0:T(8,128)(2,1)S(1)}, bf16[27,64,256]{2,1,0:T(8,128)(2,1)S(1)}, u32[]{:S(2)}, u32[]{:S(2)}) collective-permute-start(bf16[27,64,256]{2,1,0:T(8,128)(2,1)S(1)} %collective-permute-done.10.same), channel_id=1, source_target_pairs={{0,1},{1,0},{2,3},{3,2},{4,5},{5,4},{6,7},{7,6},{8,9},{9,8},{10,11... | collective-permute-start | bytes 2654216 | tf_op jit(solution)/shard_map/ppermute | solution.py:548
  59.7 14.3 %collective-permute-start.9 = (bf16[2,32,32,128]{3,2,1,0:T(8,128)(2,1)S(1)}, bf16[2,32,32,128]{3,2,1,0:T(8,128)(2,1)S(1)}, u32[]{:S(2)}, u32[]{:S(2)}) collective-permute-start(bf16[2,32,32,128]{3,2,1,0:T(8,128)(2,1)S(1)} %copy-done.3), channel_id=1, source_target_pairs={{0,16},{16,0},{1,17},{17,1},{2,18},{18,2},{3,19},{19,3},{4,20},{20... | collective-permute-start | bytes 1572872 | tf_op jit(solution)/shard_map/ppermute | solution.py:523
  61.3 12.8 %collective-permute-start.7 = (bf16[1,32,32,256]{3,2,1,0:T(8,128)(2,1)S(1)}, bf16[1,32,32,256]{3,2,1,0:T(8,128)(2,1)S(1)}, u32[]{:S(2)}, u32[]{:S(2)}) collective-permute-start(bf16[1,32,32,256]{3,2,1,0:T(8,128)(2,1)S(1)} %get-tuple-element.31.act_1.mid_1), channel_id=1, source_target_pairs={{0,1},{1,2},{2,3},{3,4},{4,5},{5,6},{6,7},{7,8},{8,9},{9,10},{10,1... | collective-permute-start | bytes 1572872 | tf_op jit(solution)/shard_map/ppermute | solution.py:526
  61.5 12.6 %collective-permute-start.8 = (bf16[1,32,32,256]{3,2,1,0:T(8,128)(2,1)S(1)}, bf16[1,32,32,256]{3,2,1,0:T(8,128)(2,1)S(1)}, u32[]{:S(2)}, u32[]{:S(2)}) collective-permute-start(bf16[1,32,32,256]{3,2,1,0:T(8,128)(2,1)S(1)} %get-tuple-element.30.act_0.mid_0), channel_id=1, source_target_pairs={{1,0},{2,1},{3,2},{4,3},{5,4},{6,5},{7,6},{8,7},{9,8},{10,9},{11,1... | collective-permute-start | bytes 1572872 | tf_op jit(solution)/shard_map/ppermute | solution.py:526
  93.2 23.0 %collective-permute-start.26 = (bf16[8,27,16,128]{3,2,1,0:T(8,128)(2,1)S(1)}, bf16[8,27,16,128]{3,2,1,0:T(8,128)(2,1)S(1)}, u32[]{:S(2)}, u32[]{:S(2)}) collective-permute-start(bf16[8,27,16,128]{3,2,1,0:T(8,128)(2,1)S(1)} %get-tuple-element.49), channel_id=1, source_target_pairs={{0,1},{1,0},{2,3},{3,2},{4,5},{5,4},{6,7},{7,6},{8,9},{9,8},{10,11... | collective-permute-start | bytes 2654216 | tf_op jit(solution)/shard_map/ppermute | solution.py:437
  116.4 13.1 %collective-permute-start.27 = (bf16[4,27,16,128]{3,2,1,0:T(8,128)(2,1)S(1)}, bf16[4,27,16,128]{3,2,1,0:T(8,128)(2,1)S(1)}, u32[]{:S(2)}, u32[]{:S(2)}) collective-permute-start(bf16[4,27,16,128]{3,2,1,0:T(8,128)(2,1)S(1)} %get-tuple-element.51), channel_id=1, source_target_pairs={{0,2},{1,3},{2,0},{3,1},{4,6},{5,7},{6,4},{7,5},{8,10},{9,11},{10,... | collective-permute-start | bytes 1327112 | tf_op jit(solution)/shard_map/ppermute | solution.py:441
  118.4 19.6 %collective-permute-start.17 = (bf16[4,27,16,128]{3,2,1,0:T(8,128)(2,1)S(1)}, bf16[4,27,16,128]{3,2,1,0:T(8,128)(2,1)S(1)}, u32[]{:S(2)}, u32[]{:S(2)}) collective-permute-start(bf16[4,27,16,128]{3,2,1,0:T(8,128)(2,1)S(1)} %get-tuple-element.43), channel_id=1, source_target_pairs={{0,2},{1,3},{2,0},{3,1},{4,6},{5,7},{6,4},{7,5},{8,10},{9,11},{10,... | collective-permute-start | bytes 1327112 | tf_op jit(solution)/shard_map/ppermute | solution.py:441
  129.6 12.1 %collective-permute-start.28 = (bf16[27,16,128]{2,1,0:T(8,128)(2,1)S(1)}, bf16[27,16,128]{2,1,0:T(8,128)(2,1)S(1)}, u32[]{:S(2)}, u32[]{:S(2)}) collective-permute-start(bf16[27,16,128]{2,1,0:T(8,128)(2,1)S(1)} %get-tuple-element.53), channel_id=1, source_target_pairs={{0,4},{1,5},{2,6},{3,7},{4,8},{5,9},{6,10},{7,11},{8,12},{9,13},{1... | collective-permute-start | bytes 331784 | tf_op jit(solution)/shard_map/ppermute | solution.py:445
  129.6 12.4 %collective-permute-start.29 = (bf16[27,16,128]{2,1,0:T(8,128)(2,1)S(1)}, bf16[27,16,128]{2,1,0:T(8,128)(2,1)S(1)}, u32[]{:S(2)}, u32[]{:S(2)}) collective-permute-start(bf16[27,16,128]{2,1,0:T(8,128)(2,1)S(1)} %get-tuple-element.54), channel_id=1, source_target_pairs={{0,8},{1,9},{2,10},{3,11},{4,12},{5,13},{6,14},{7,15},{8,0},{9,1},... | collective-permute-start | bytes 331784 | tf_op jit(solution)/shard_map/ppermute | solution.py:445
  138.2 13.7 %collective-permute-start.19 = (bf16[27,16,128]{2,1,0:T(8,128)(2,1)S(1)}, bf16[27,16,128]{2,1,0:T(8,128)(2,1)S(1)}, u32[]{:S(2)}, u32[]{:S(2)}) collective-permute-start(bf16[27,16,128]{2,1,0:T(8,128)(2,1)S(1)} %get-tuple-element.46), channel_id=1, source_target_pairs={{0,8},{1,9},{2,10},{3,11},{4,12},{5,13},{6,14},{7,15},{8,0},{9,1},... | collective-permute-start | bytes 331784 | tf_op jit(solution)/shard_map/ppermute | solution.py:445
  142.1 16.3 %collective-permute-start.33 = (bf16[27,16,128]{2,1,0:T(8,128)(2,1)S(1)}, bf16[27,16,128]{2,1,0:T(8,128)(2,1)S(1)}, u32[]{:S(2)}, u32[]{:S(2)}) collective-permute-start(bf16[27,16,128]{2,1,0:T(8,128)(2,1)S(1)} %sum_two_level.1.own), channel_id=1, source_target_pairs={{0,12},{1,13},{2,14},{3,15},{4,0},{5,1},{6,2},{7,3},{8,4},{9,5},{1... | collective-permute-start | bytes 331784 | tf_op jit(solution)/shard_map/ppermute | solution.py:449
  144.2 21.5 %collective-permute-start.32 = (bf16[27,16,128]{2,1,0:T(8,128)(2,1)S(1)}, bf16[27,16,128]{2,1,0:T(8,128)(2,1)S(1)}, u32[]{:S(2)}, u32[]{:S(2)}) collective-permute-start(bf16[27,16,128]{2,1,0:T(8,128)(2,1)S(1)} %sum_two_level.1.own), channel_id=1, source_target_pairs={{0,8},{1,9},{2,10},{3,11},{4,12},{5,13},{6,14},{7,15},{8,0},{9,1},... | collective-permute-start | bytes 331784 | tf_op jit(solution)/shard_map/ppermute | solution.py:449
  146.0 19.6 %collective-permute-start.31 = (bf16[27,16,128]{2,1,0:T(8,128)(2,1)S(1)}, bf16[27,16,128]{2,1,0:T(8,128)(2,1)S(1)}, u32[]{:S(2)}, u32[]{:S(2)}) collective-permute-start(bf16[27,16,128]{2,1,0:T(8,128)(2,1)S(1)} %sum_two_level.1.own), channel_id=1, source_target_pairs={{0,4},{1,5},{2,6},{3,7},{4,8},{5,9},{6,10},{7,11},{8,12},{9,13},{1... | collective-permute-start | bytes 331784 | tf_op jit(solution)/shard_map/ppermute | solution.py:449
  152.0 15.3 %collective-permute-start.23 = (bf16[27,16,128]{2,1,0:T(8,128)(2,1)S(1)}, bf16[27,16,128]{2,1,0:T(8,128)(2,1)S(1)}, u32[]{:S(2)}, u32[]{:S(2)}) collective-permute-start(bf16[27,16,128]{2,1,0:T(8,128)(2,1)S(1)} %sum_one_level.1.own), channel_id=1, source_target_pairs={{0,12},{1,13},{2,14},{3,15},{4,0},{5,1},{6,2},{7,3},{8,4},{9,5},{1... | collective-permute-start | bytes 331784 | tf_op jit(solution)/shard_map/ppermute | solution.py:449
  158.4 11.9 %collective-permute-start.22 = (bf16[27,16,128]{2,1,0:T(8,128)(2,1)S(1)}, bf16[27,16,128]{2,1,0:T(8,128)(2,1)S(1)}, u32[]{:S(2)}, u32[]{:S(2)}) collective-permute-start(bf16[27,16,128]{2,1,0:T(8,128)(2,1)S(1)} %sum_one_level.1.own), channel_id=1, source_target_pairs={{0,8},{1,9},{2,10},{3,11},{4,12},{5,13},{6,14},{7,15},{8,0},{9,1},... | collective-permute-start | bytes 331784 | tf_op jit(solution)/shard_map/ppermute | solution.py:449
  165.7 13.1 %collective-permute-start.34 = (bf16[4,27,16,128]{3,2,1,0:T(8,128)(2,1)S(1)}, bf16[4,27,16,128]{3,2,1,0:T(8,128)(2,1)S(1)}, u32[]{:S(2)}, u32[]{:S(2)}) collective-permute-start(bf16[4,27,16,128]{3,2,1,0:T(8,128)(2,1)S(1)} %sum_two_levels.1.own), channel_id=1, source_target_pairs={{0,2},{1,3},{2,0},{3,1},{4,6},{5,7},{6,4},{7,5},{8,10},{9,11},{10,... | collective-permute-start | bytes 1327112 | tf_op jit(solution)/shard_map/ppermute | solution.py:451
  170.4 17.0 %collective-permute-start.24 = (bf16[4,27,16,128]{3,2,1,0:T(8,128)(2,1)S(1)}, bf16[4,27,16,128]{3,2,1,0:T(8,128)(2,1)S(1)}, u32[]{:S(2)}, u32[]{:S(2)}) collective-permute-start(bf16[4,27,16,128]{3,2,1,0:T(8,128)(2,1)S(1)} %sum_one_levels.1.own), channel_id=1, source_target_pairs={{0,2},{1,3},{2,0},{3,1},{4,6},{5,7},{6,4},{7,5},{8,10},{9,11},{10,... | collective-permute-start | bytes 1327112 | tf_op jit(solution)/shard_map/ppermute | solution.py:451
  178.9 29.8 %collective-permute-start.35 = (bf16[8,27,16,128]{3,2,1,0:T(8,128)(2,1)S(1)}, bf16[8,27,16,128]{3,2,1,0:T(8,128)(2,1)S(1)}, u32[]{:S(2)}, u32[]{:S(2)}) collective-permute-start(bf16[8,27,16,128]{3,2,1,0:T(8,128)(2,1)S(1)} %sum_two_sides.1.own), channel_id=1, source_target_pairs={{0,1},{1,0},{2,3},{3,2},{4,5},{5,4},{6,7},{7,6},{8,9},{9,8},{10,11... | collective-permute-start | bytes 2654216 | tf_op jit(solution)/shard_map/ppermute | solution.py:453
  187.5 23.3 %collective-permute-start.25 = (bf16[8,27,16,128]{3,2,1,0:T(8,128)(2,1)S(1)}, bf16[8,27,16,128]{3,2,1,0:T(8,128)(2,1)S(1)}, u32[]{:S(2)}, u32[]{:S(2)}) collective-permute-start(bf16[8,27,16,128]{3,2,1,0:T(8,128)(2,1)S(1)} %sum_one_sides.1.own), channel_id=1, source_target_pairs={{0,1},{1,0},{2,3},{3,2},{4,5},{5,4},{6,7},{7,6},{8,9},{9,8},{10,11... | collective-permute-start | bytes 2654216 | tf_op jit(solution)/shard_map/ppermute | solution.py:453
  (16 other events, 220.1 us)
where the time goes:
time: 216 us; the launch traced here: 213 us
  waiting for transfers between devices  101 us (47%)
  Pallas kernels  55.2 us (26%)
  starting transfers between devices  54.4 us (25%)
    pallas_call x4, Pallas kernels, conv_call(): pl.pallas_call(kernel, out_shape=[jax.ShapeDtypeStruct(shape, jnp.bfloat1...  37.6 us
    ppermute x4, waiting for transfers between devices, other(): return lax.ppermute(values, 'chan', across)  36.6 us
    ppermute x10, waiting for transfers between devices, rims(): return (lax.ppermute(last, 'dp', ahead), lax.ppermute(first, 'dp', behind))  21.5 us
    ppermute x10, starting transfers between devices, rims(): return (lax.ppermute(last, 'dp', ahead), lax.ppermute(first, 'dp', behind))  16.7 us
    ppermute x6, starting transfers between devices, layer_sum(): came = [lax.ppermute(own, 'dp', pairs) for pairs in levels]  16.1 us
    ppermute x2, waiting for transfers between devices, layer_sum(): came = lax.ppermute(own, 'dp', sides)  15.3 us
    ppermute x2, waiting for transfers between devices, layer_sum(): came = lax.ppermute(send, 'dp', sides)  15.3 us
    pallas_call x2, Pallas kernels, filter_call(): pl.pallas_call(filter_kernel, grid=(1,), out_shape=[jax.ShapeDtypeStruct(...  12.3 us
  transfers between devices with their start and end apart: 36, of which 17 were waited for; matrix products, arithmetic and copies ran while one was open for 0% of the time, Pallas kernels for 20%

commit v1 on v0

--- a/solution.py
+++ b/solution.py
@@ -13,7 +13,7 @@
 HALF = 128
 FULL = 256
 TILE = 16
-VMEM_LIMIT = 40 * 1024 * 1024
+VMEM_LIMIT = 32 * 1024 * 1024
 
 
 def extended(block, sides, width):
@@ -135,45 +135,84 @@
     return (output, input_grad, summed_one * scale, summed_two * scale)
 
 
-def copy_weights(own_ref, same_ref, swap_ref, full_ref, sems):
+def is_seam():
+    return lax.rem(lax.axis_index("dp") * 2, VOX) == 0
+
+
+def place():
+    at = lax.axis_index("dp")
+    return at // 4, lax.rem(at // 2, 2), lax.rem(at, 2)
+
+
+def shaped(values):
+    return values.reshape(TILE, VOX, values.shape[1])
+
+
+PARTS = {
+    "all": dict(
+        slots=((0, True), (1, True), (2, False), (1, False), (2, True), (3, True)),
+        taps=(((0, 0), (1, 1), (2, 2)), ((0, 3), (1, 4), (2, 5))),
+        depths=(0, 1, 2),
+    ),
+    "local": dict(
+        slots=((0, True), (1, True), (0, False), (1, False)),
+        taps=(((1, 0), (2, 3)), ((0, 2), (1, 1))),
+        depths=(0, 1, 2),
+    ),
+    "rim": dict(
+        slots=((0, True), (1, True)),
+        taps=(((0, 0),), ((2, 1),)),
+        depths=(0, 2),
+    ),
+}
+
+
+def filter_rows(kind):
+    _, side, core = place()
+    if kind == "own":
+        return [(HALF, 0)]
+    if kind == "quarters":
+        return [
+            (32, (2 * along + unit) * 32)
+            for unit in (core, 1 - core)
+            for along in (side, 1 - side)
+        ]
+    return [(HALF, 0), (64, HALF + core * 64), (64, HALF + (1 - core) * 64)]
+
+
+def copy_weights(kind, part, pieces, store, sems):
     me = lax.axis_index("chan")
-    core = lax.rem(lax.axis_index("dp"), 2)
-    quarter = HALF // 2
-    sources = [(own_ref, HALF, 0)]
-    if same_ref is not None:
-        sources.append((same_ref, quarter, HALF + core * quarter))
-        sources.append((swap_ref, quarter, HALF + (1 - core) * quarter))
     copies = []
-    for source, height, row in sources:
+    for (height, row), piece in zip(filter_rows(kind), pieces):
+        if not isinstance(row, int):
+            row = pl.multiple_of(row, 32)
+        spans = ((0, 27),) if part != "rim" else ((0, 9), (18, 9))
         for side in range(2):
             column = pl.multiple_of((me if side == 0 else 1 - me) * HALF, HALF)
-            if not isinstance(row, int):
-                row = pl.multiple_of(row, quarter)
-            copies.append(
-                pltpu.make_async_copy(
-                    source.at[:, :, pl.ds(column, HALF)],
-                    full_ref.at[:, pl.ds(row, height), pl.ds(side * HALF, HALF)],
-                    sems.at[len(copies)],
+            for first, length in spans:
+                taps = pl.ds(first, length)
+                copies.append(
+                    pltpu.make_async_copy(
+                        piece.at[taps, :, pl.ds(column, HALF)],
+                        store.at[taps, pl.ds(row, height), pl.ds(side * HALF, HALF)],
+                        sems.at[len(copies)],
+                    )
                 )
-            )
     for copy in copies:
         copy.start()
     return copies
 
 
-def is_seam():
-    return lax.rem(lax.axis_index("dp") * 2, VOX) == 0
-
-
-def fill_planes(planes, store):
-    for slot in range(6):
-        store[slot, 0] = jnp.zeros(store.shape[2:], store.dtype)
-        store[slot, VOX + 1] = jnp.zeros(store.shape[2:], store.dtype)
-    for slot, plane in ((0, 0), (1, 1), (4, 2), (5, 3)):
-        for lane, ref, at in planes[plane]:
-            store[slot, 1 : VOX + 1, :, lane : lane + ref.shape[3]] = ref[at]
+def fill_planes(part, planes, store):
+    edge = jnp.zeros(store.shape[2:], store.dtype)
     seam = is_seam()
-    for slot, plane in ((2, 2), (3, 1)):
+    for slot, (plane, always) in enumerate(PARTS[part]["slots"]):
+        ref, at = planes[plane]
+        store[slot, 0] = edge
+        store[slot, VOX + 1] = edge
+        if always:
+            store[slot, 1 : VOX + 1] = ref[at]
+            continue
 
         @pl.when(seam)
         def _():
@@ -181,29 +220,28 @@
 
         @pl.when(jnp.logical_not(seam))
         def _():
-            for lane, ref, at in planes[plane]:
-                store[slot, 1 : VOX + 1, :, lane : lane + ref.shape[3]] = ref[at]
-
-
-def conv_rows(store, weights, plane, row, flipped):
+            store[slot, 1 : VOX + 1] = ref[at]
+
+
+def conv_rows(store, weights, taps, row, flipped):
     pieces = []
-    for a in range(3):
+    for _, slot in taps:
         for b in range(3):
-            piece = store[3 * plane + a, pl.ds(row + b, TILE)]
-            pieces.append(piece.reshape(TILE * VOX, FULL))
+            piece = store[slot, pl.ds(row + b, TILE)]
+            pieces.append(piece.reshape(TILE * VOX, store.shape[3]))
     stacked = jnp.concatenate(pieces, axis=1)
     products = []
     for c in range(3):
         if flipped:
-            taps = [weights[(2 - a) * 9 + (2 - b) * 3 + 2 - c] for a in range(3) for b in range(3)]
+            tiles = [weights[(2 - a) * 9 + (2 - b) * 3 + 2 - c] for a, _ in taps for b in range(3)]
             dims = (((1,), (1,)), ((), ()))
-            taps = jnp.concatenate(taps, axis=1)
+            tiles = jnp.concatenate(tiles, axis=1)
         else:
-            taps = [weights[a * 9 + b * 3 + c] for a in range(3) for b in range(3)]
+            tiles = [weights[a * 9 + b * 3 + c] for a, _ in taps for b in range(3)]
             dims = (((1,), (0,)), ((), ()))
-            taps = jnp.concatenate(taps, axis=0)
+            tiles = jnp.concatenate(tiles, axis=0)
         products.append(
-            lax.dot_general(stacked, taps, dims, preferred_element_type=jnp.float32)
+            lax.dot_general(stacked, tiles, dims, preferred_element_type=jnp.float32)
         )
     left, middle, right = products
     column = lax.rem(lax.broadcasted_iota(jnp.int32, left.shape, 0), VOX)
@@ -212,100 +250,57 @@
     return middle + left + right
 
 
-def over_tiles(body):
+def conv_kernel(part, kind, flipped, finish, counts, *refs):
+    refs = list(refs)
+    groups = []
+    for count in counts:
+        groups.append(refs[:count])
+        refs = refs[count:]
+    planes, pieces, begun, extra, outs = groups
+    weights, store, sems = refs
+    copies = copy_weights(kind, part, pieces, weights, sems)
+    views = []
+    for ref in planes:
+        views += [(ref, at) for at in range(ref.shape[0])]
+    fill_planes(part, views, store)
+    for copy in copies:
+        copy.wait()
     for plane in range(2):
+        taps = PARTS[part]["taps"][plane]
 
         @pl.loop(0, VOX // TILE)
         def _(step):
-            body(plane, pl.multiple_of(step * TILE, TILE))
-
-
-def shaped(values):
-    return values.reshape(TILE, VOX, values.shape[1])
-
-
-def first_kernel(
-    mid_own, mid_other, low_own, high_own, low_other, high_other, own, same, swap,
-    act_0, act_1, weights, store, sems,
-):
-    copies = copy_weights(own, same, swap, weights, sems)
-    fill_planes(
-        [
-            ((0, low_own, 0), (HALF, low_other, 0)),
-            ((0, mid_own, 0), (HALF, mid_other, 0)),
-            ((0, mid_own, 1), (HALF, mid_other, 1)),
-            ((0, high_own, 0), (HALF, high_other, 0)),
-        ],
-        store,
-    )
-    for copy in copies:
-        copy.wait()
-
-    def body(plane, row):
-        value = leaky(conv_rows(store, weights, plane, row, False))
-        target = (act_0, act_1)[plane]
-        target[0, pl.ds(row, TILE)] = shaped(value.astype(jnp.bfloat16))
-
-    over_tiles(body)
-
-
-def second_kernel(
-    act_0, act_1, low, high, cot_own, cot_other, own, same, swap,
-    output, delta_0, delta_1, weights, store, sems,
-):
-    copies = copy_weights(own, same, swap, weights, sems)
-    fill_planes(
-        [((0, low, 0),), ((0, act_0, 0),), ((0, act_1, 0),), ((0, high, 0),)], store
-    )
-    for copy in copies:
-        copy.wait()
-
-    def body(plane, row):
-        value = conv_rows(store, weights, plane, row, False)
-        output[plane, pl.ds(row, TILE)] = shaped(leaky(value[:, :HALF]).astype(jnp.bfloat16))
-        slope = slope_of(value)
-        target = (delta_0, delta_1)[plane]
-        for lane, cot in ((0, cot_own), (HALF, cot_other)):
-            grad = cot[plane, pl.ds(row, TILE)].astype(jnp.float32)
-            delta = grad * shaped(slope[:, lane : lane + HALF])
-            target[0, pl.ds(row, TILE), :, lane : lane + HALF] = delta.astype(jnp.bfloat16)
-
-    over_tiles(body)
-
-
-def back_kernel(
-    delta_0, delta_1, low, high, act_0, act_1, own, same, swap,
-    prior_0, prior_1, weights, store, sems,
-):
-    copies = copy_weights(own, same, swap, weights, sems)
-    fill_planes(
-        [((0, low, 0),), ((0, delta_0, 0),), ((0, delta_1, 0),), ((0, high, 0),)], store
-    )
-    for copy in copies:
-        copy.wait()
-
-    def body(plane, row):
-        value = shaped(conv_rows(store, weights, plane, row, True))
-        act = (act_0, act_1)[plane][0, pl.ds(row, TILE)].astype(jnp.float32)
-        target = (prior_0, prior_1)[plane]
-        target[0, pl.ds(row, TILE)] = (value * slope_of(act)).astype(jnp.bfloat16)
-
-    over_tiles(body)
-
-
-def last_kernel(delta_0, delta_1, low, high, own, grad, weights, store, sems):
-    copies = copy_weights(own, None, None, weights, sems)
-    fill_planes(
-        [((0, low, 0),), ((0, delta_0, 0),), ((0, delta_1, 0),), ((0, high, 0),)], store
-    )
-    for copy in copies:
-        copy.wait()
-
-    def body(plane, row):
-        value = conv_rows(store, weights, plane, row, True)
-        grad[plane, pl.ds(row, TILE)] = shaped(value.astype(jnp.bfloat16))
-
-    over_tiles(body)
+            rows = pl.ds(pl.multiple_of(step * TILE, TILE), TILE)
+            value = shaped(conv_rows(store, weights, taps, step * TILE, flipped))
+            if begun:
+                value = value + begun[0][plane, rows]
+            finish(value, plane, rows, extra, outs)
+
+
+def finish_partial(value, plane, rows, extra, outs):
+    outs[0][plane, rows] = value
+
+
+def finish_first(value, plane, rows, extra, outs):
+    outs[plane][0, rows] = leaky(value).astype(jnp.bfloat16)
+
+
+def finish_second(value, plane, rows, extra, outs):
+    output, deltas = outs[0], outs[1:]
+    output[plane, rows] = leaky(value[:, :, :HALF]).astype(jnp.bfloat16)
+    slope = slope_of(value)
+    for lane, cot in ((0, extra[0]), (HALF, extra[1])):
+        delta = cot[plane, rows].astype(jnp.float32) * slope[:, :, lane : lane + HALF]
+        deltas[plane][0, rows, :, lane : lane + HALF] = delta.astype(jnp.bfloat16)
+
+
+def finish_back(value, plane, rows, extra, outs):
+    act = extra[plane][0, rows].astype(jnp.float32)
+    outs[plane][0, rows] = (value * slope_of(act)).astype(jnp.bfloat16)
+
+
+def finish_last(value, plane, rows, extra, outs):
+    outs[0][plane, rows] = value.astype(jnp.bfloat16)
 
 
 def filter_kernel(low, mid_0, mid_1, high, delta_0, delta_1, keep, send, turned, moved):
@@ -356,11 +351,6 @@
                 send[:, tap] = sent[rows].reshape(8, 16, HALF).astype(send.dtype)
 
 
-def place():
-    at = lax.axis_index("dp")
-    return at // 4, lax.rem(at // 2, 2), lax.rem(at, 2)
-
-
 def add_core_kernel(keep, came, kept, sent):
     _, side, _ = place()
     for target, first in ((kept, side * 4), (sent, (1 - side) * 4)):
@@ -426,53 +416,70 @@
     )(*operands)
 
 
-def layer_sum(keep, send, scale, name):
+PART = (27, 16, HALF)
+
+
+def to_levels(blocks):
     count = lax.axis_size("dp")
-    wide, thin = jnp.float32, jnp.bfloat16
-    cores = [(i, i ^ 1) for i in range(count)]
-    sides = [(i, i ^ 2) for i in range(count)]
-    levels = [[(i, (i + 4 * step) % count) for i in range(count)] for step in (1, 2, 3)]
-    part = (27, 16, HALF)
-
-    came = lax.ppermute(send, "dp", cores)
-    keep, send = small_call(
-        add_core_kernel, [((4,) + part, wide), ((4,) + part, thin)], [keep, came], name + "_core"
-    )
-    came = lax.ppermute(send, "dp", sides)
-    keep, *sends = small_call(
-        add_side_kernel, [(part, wide)] + [(part, thin)] * 3, [keep, came], name + "_side"
-    )
-    came = [lax.ppermute(block, "dp", pairs) for block, pairs in zip(sends, levels)]
-    (own,) = small_call(
-        functools.partial(add_level_kernel, scale), [(part, thin)], [keep, *came], name + "_level"
-    )
-    came = [lax.ppermute(own, "dp", pairs) for pairs in levels]
-    (own,) = small_call(join_level_kernel, [((4,) + part, thin)], [own, *came], name + "_levels")
-    came = lax.ppermute(own, "dp", sides)
-    (own,) = small_call(join_side_kernel, [((8,) + part, thin)], [own, came], name + "_sides")
-    came = lax.ppermute(own, "dp", cores)
-    (grad,) = small_call(join_core_kernel, [((27, HALF, FULL), wide)], [own, came], name + "_cores")
-    return grad
-
-
-def conv_call(kernel, outs, operands, weight_rows, name):
-    flops = 2 * 2 * VOX * VOX * 27 * FULL * weight_rows
-    count = sum(ref.size * 2 for ref in operands)
-    narrow = weight_rows == HALF
-    specs = [pl.BlockSpec(memory_space=pltpu.VMEM)] * (len(operands) - (1 if narrow else 3))
-    specs += [pl.BlockSpec(memory_space=pl.ANY)] * (1 if narrow else 3)
+    return [
+        lax.ppermute(block, "dp", [(i, (i + 4 * step) % count) for i in range(count)])
+        for step, block in enumerate(blocks, 1)
+    ]
+
+
+def sum_core(keep, came, name):
+    outs = [((4,) + PART, jnp.float32), ((4,) + PART, jnp.bfloat16)]
+    return small_call(add_core_kernel, outs, [keep, came], name + "_core")
+
+
+def sum_side(keep, came, name):
+    outs = [(PART, jnp.float32)] + [(PART, jnp.bfloat16)] * 3
+    return small_call(add_side_kernel, outs, [keep, came], name + "_side")
+
+
+def sum_level(keep, came, scale, name):
+    kernel = functools.partial(add_level_kernel, scale)
+    return small_call(kernel, [(PART, jnp.bfloat16)], [keep, *came], name + "_level")[0]
+
+
+def join_level(own, came, name):
+    outs = [((4,) + PART, jnp.bfloat16)]
+    return small_call(join_level_kernel, outs, [own, *came], name + "_levels")[0]
+
+
+def join_side(own, came, name):
+    outs = [((8,) + PART, jnp.bfloat16)]
+    return small_call(join_side_kernel, outs, [own, came], name + "_sides")[0]
+
+
+def join_core(own, came, name):
+    outs = [((27, HALF, FULL), jnp.float32)]
+    return small_call(join_core_kernel, outs, [own, came], name + "_cores")[0]
+
+
+def conv_call(name, part, kind, finish, outs, planes, pieces, begun=(), extra=(), flipped=False):
+    lanes = planes[0].shape[3]
+    height = {"own": HALF, "quarters": HALF, "both": FULL}[kind]
+    depths = len(PARTS[part]["taps"][0])
+    flops = 2 * 2 * VOX * VOX * 9 * depths * FULL * height
+    operands = [*planes, *pieces, *begun, *extra]
+    moved = sum(ref.size * ref.dtype.itemsize for ref in operands)
+    counts = (len(planes), len(pieces), len(begun), len(extra), len(outs))
+    specs = [pl.BlockSpec(memory_space=pltpu.VMEM) for _ in operands]
+    for at in range(len(planes), len(planes) + len(pieces)):
+        specs[at] = pl.BlockSpec(memory_space=pl.ANY)
     return pl.pallas_call(
-        kernel,
-        out_shape=[jax.ShapeDtypeStruct(shape, jnp.bfloat16) for shape in outs],
+        functools.partial(conv_kernel, part, kind, flipped, finish, counts),
+        out_shape=[jax.ShapeDtypeStruct(shape, dtype) for shape, dtype in outs],
         in_specs=specs,
         out_specs=[pl.BlockSpec(memory_space=pltpu.VMEM)] * len(outs),
         scratch_shapes=[
-            pltpu.VMEM((27, weight_rows, FULL), jnp.bfloat16),
-            pltpu.VMEM((6, VOX + 2, VOX, FULL), jnp.bfloat16),
-            pltpu.SemaphoreType.DMA((6,)),
+            pltpu.VMEM((27, height, FULL), jnp.bfloat16),
+            pltpu.VMEM((len(PARTS[part]["slots"]), VOX + 2, VOX, lanes), jnp.bfloat16),
+            pltpu.SemaphoreType.DMA((16,)),
         ],
         compiler_params=pltpu.CompilerParams(vmem_limit_bytes=VMEM_LIMIT),
-        cost_estimate=pl.CostEstimate(flops=flops, bytes_accessed=count, transcendentals=0),
+        cost_estimate=pl.CostEstimate(flops=flops, bytes_accessed=moved, transcendentals=0),
         name=name,
     )(*operands)
 
@@ -512,74 +519,106 @@
     count = lax.axis_size("dp")
     ahead = [(i, (i + 1) % count) for i in range(count)]
     behind = [(target, source) for source, target in ahead]
-    cores = [(i, i ^ 1) for i in range(count)]
-    across = [(0, 1), (1, 0)]
-    core = lax.rem(lax.axis_index("dp"), 2)
     scale = 1.0 / math.sqrt(count * 2 * VOX * VOX)
     one = filter_one.reshape(27, HALF, FULL)
     two = filter_two.reshape(27, HALF, FULL)
+    _, side, core = place()
 
     def other(values):
-        return lax.ppermute(values, "chan", across)
+        return lax.ppermute(values, "chan", [(0, 1), (1, 0)])
+
+    def to_core(values):
+        return lax.ppermute(values, "dp", [(i, i ^ 1) for i in range(count)])
+
+    def to_side(values):
+        return lax.ppermute(values, "dp", [(i, i ^ 2) for i in range(count)])
 
     def rims(first, last):
         return lax.ppermute(last, "dp", ahead), lax.ppermute(first, "dp", behind)
 
-    def my_part(weight):
-        return lax.dynamic_slice_in_dim(weight, core * (HALF // 2), HALF // 2, axis=1)
-
-    volume_other = other(volume)
+    wide = ((1, VOX, VOX, FULL), jnp.bfloat16)
+    narrow = ((2, VOX, VOX, HALF), jnp.bfloat16)
+    partial = ((2, VOX, VOX, FULL), jnp.float32)
+
+    one_0 = other(lax.dynamic_slice_in_dim(one, (2 * side + core) * 32, 32, axis=1))
     low_own, high_own = rims(volume[:1], volume[1:])
-    one_same = other(my_part(one))
+    one_1 = to_side(one_0)
+    one_2 = to_core(one_0)
+    volume_other = other(after(volume, one_0))
+    two_same = other(
+        after(lax.dynamic_slice_in_dim(two, core * 64, 64, axis=1), volume_other)
+    )
     low_other, high_other = rims(volume_other[:1], volume_other[1:])
-    one_swap = lax.ppermute(one_same, "dp", cores)
-    two_same = other(after(my_part(two), one_same))
-    cot_other = other(after(cotangent, one_same))
-    wide = (1, VOX, VOX, FULL)
-    narrow = (2, VOX, VOX, HALF)
+    one_3 = to_core(one_1)
+    quarters = [one_0, one_1, one_2, one_3]
+
+    (begun,) = conv_call(
+        "first_own", "all", "own", finish_partial, [partial], [low_own, volume, high_own], [one]
+    )
+    (begun,) = conv_call(
+        "first_other", "local", "quarters", finish_partial, [partial], [volume_other], quarters,
+        [begun],
+    )
+    cot_other = other(after(cotangent, low_other))
     act_0, act_1 = conv_call(
-        first_kernel,
-        [wide, wide],
-        [volume, volume_other, low_own, high_own, low_other, high_other, one, one_same, one_swap],
-        FULL,
-        "first_layer",
+        "first_rim", "rim", "quarters", finish_first, [wide, wide], [low_other, high_other],
+        quarters, [begun],
     )
     low_act, high_act = rims(act_0, act_1)
-    two_swap = lax.ppermute(after(two_same, act_0), "dp", cores)
+    two_swap = to_core(after(two_same, act_0))
+    pieces = [two, two_same, two_swap]
+    (begun,) = conv_call(
+        "second_local", "local", "both", finish_partial, [partial], [act_0, act_1], pieces
+    )
     output, delta_0, delta_1 = conv_call(
-        second_kernel,
-        [narrow, wide, wide],
-        [act_0, act_1, low_act, high_act, cotangent, cot_other, two, two_same, two_swap],
-        FULL,
-        "second_layer",
+        "second_rim", "rim", "both", finish_second, [narrow, wide, wide], [low_act, high_act],
+        pieces, [begun], [cotangent, cot_other],
     )
     low_delta, high_delta = rims(delta_0, delta_1)
-    local_two = filter_call(
+    keep, send = filter_call(
         [low_act, act_0, act_1, high_act], (0, 0, 0, 0), [delta_0, delta_1], "grad_two"
     )
-    summed_two = layer_sum(*local_two, scale, "sum_two")
+    came_two = to_core(send)
+    (begun,) = conv_call(
+        "back_local", "local", "both", finish_partial, [partial], [delta_0, delta_1], pieces,
+        flipped=True,
+    )
+    keep_two, send_two = sum_core(keep, came_two, "sum_two")
     prior_0, prior_1 = conv_call(
-        back_kernel,
-        [wide, wide],
-        [delta_0, delta_1, low_delta, high_delta, act_0, act_1, two, two_same, two_swap],
-        FULL,
-        "second_back",
-    )
+        "back_rim", "rim", "both", finish_back, [wide, wide], [after(low_delta, keep_two), high_delta],
+        pieces, [begun], [act_0, act_1], flipped=True,
+    )
+    came_two = to_side(send_two)
     low_prior, high_prior = rims(prior_0, prior_1)
-    local_one = filter_call(
+    keep, send = filter_call(
         [low_own, volume, volume, high_own], (0, 0, 1, 0), [prior_0, prior_1], "grad_one"
     )
-    summed_one = layer_sum(*local_one, scale, "sum_one")
+    came_one = to_core(send)
+    keep_two, *sends_two = sum_side(keep_two, came_two, "sum_two")
+    keep_one, send_one = sum_core(keep, after(came_one, keep_two), "sum_one")
+    came_two = to_levels(sends_two)
+    came_one = to_side(send_one)
+    own_two = sum_level(keep_two, came_two, scale, "sum_two")
+    keep_one, *sends_one = sum_side(keep_one, after(came_one, own_two), "sum_one")
+    came_one = to_levels(sends_one)
+    came_two = to_levels([own_two] * 3)
     (input_grad,) = conv_call(
-        last_kernel, [narrow], [prior_0, prior_1, low_prior, high_prior, one], HALF, "first_back"
-    )
+        "first_back", "all", "own", finish_last, [narrow], [low_prior, prior_0, prior_1, high_prior],
+        [one], flipped=True,
+    )
+    own_one = sum_level(after(keep_one, input_grad), came_one, scale, "sum_one")
+    own_two = join_level(own_two, came_two, "sum_two")
+    came_one = to_levels([after(own_one, own_two)] * 3)
+    came_two = to_side(own_two)
+    own_two = join_side(own_two, came_two, "sum_two")
+    own_one = join_level(own_one, [after(came_one[0], own_two)] + came_one[1:], "sum_one")
+    came_one = to_side(own_one)
+    came_two = to_core(own_two)
+    summed_two = join_core(own_two, came_two, "sum_two")
+    own_one = join_side(own_one, after(came_one, summed_two), "sum_one")
+    summed_one = join_core(own_one, to_core(own_one), "sum_one")
     shape = filter_one.shape
-    return (
-        output,
-        input_grad,
-        summed_one.reshape(shape),
-        summed_two.reshape(shape),
-    )
+    return output, input_grad, summed_one.reshape(shape), summed_two.reshape(shape)
 
 
 def local(volume, filter_one, filter_two, cotangent):

time: 216 us -> 211 us (0.977)
  waiting for transfers between devices: 101 us -> 84.7 us
  Pallas kernels: 55.2 us -> 64.6 us
    ppermute x10, waiting for transfers between devices: 21.5 us -> 0.03 us  [rims(): return (lax.ppermute(last, 'dp', ahead), lax.ppermute(first, 'dp', behind))]
    pallas_call x4 -> x8, Pallas kernels: 37.6 us -> 46.1 us  [conv_call(): pl.pallas_call(functools.partial(conv_kernel, part, kind, flipped, finish...]
    ppermute x26 -> x28, waiting for transfers between devices: 79.4 us -> 84.6 us  [the longest x5 51.1 us: to_side(): return lax.ppermute(values, 'dp', [(i, i ^ 2) for i in range(count)])]
    ppermute x10, starting transfers between devices: 16.7 us -> 20.9 us  [rims(): return (lax.ppermute(last, 'dp', ahead), lax.ppermute(first, 'dp', behind))]
    ppermute x26 -> x28, starting transfers between devices: 37.8 us -> 34.2 us  [the longest x12 17.5 us: to_levels(): lax.ppermute(block, 'dp', [(i, (i + 4 * step) % count) for i in range(cou...]
  transfers between devices with their start and end apart: 36 -> 38, of which waited for: 17 -> 16; matrix products, arithmetic and copies ran while one was open for 0% -> 1% of each run, Pallas kernels for 20% -> 19%
where the time goes in v1:
time: 211 us; the launch traced here: 209 us
  waiting for transfers between devices  84.7 us (40%)
  Pallas kernels  64.6 us (31%)
  starting transfers between devices  55.1 us (26%)
  local copies, waits for them, and re-layouts  3.17 us (2%)
    ppermute x5, waiting for transfers between devices, to_side(): return lax.ppermute(values, 'dp', [(i, i ^ 2) for i in range(count)])  51.1 us
    pallas_call x8, Pallas kernels, conv_call(): pl.pallas_call(functools.partial(conv_kernel, part, kind, flipped, finish...  46.1 us
    ppermute x10, starting transfers between devices, rims(): return (lax.ppermute(last, 'dp', ahead), lax.ppermute(first, 'dp', behind))  20.9 us
    ppermute x12, waiting for transfers between devices, to_levels(): lax.ppermute(block, 'dp', [(i, (i + 4 * step) % count) for i in range(cou...  17.8 us
    ppermute x12, starting transfers between devices, to_levels(): lax.ppermute(block, 'dp', [(i, (i + 4 * step) % count) for i in range(cou...  17.5 us
    ppermute x4, waiting for transfers between devices, other(): return lax.ppermute(values, 'chan', [(0, 1), (1, 0)])  13.3 us
    pallas_call x2, Pallas kernels, filter_call(): pl.pallas_call(filter_kernel, grid=(1,), out_shape=[jax.ShapeDtypeStruct(...  13.3 us
    ppermute x7, starting transfers between devices, to_core(): return lax.ppermute(values, 'dp', [(i, i ^ 1) for i in range(count)])  6.25 us
  transfers between devices with their start and end apart: 38, of which 16 were waited for; matrix products, arithmetic and copies ran while one was open for 1% of the time, Pallas kernels for 19%

profile of v1, /device:TPU:0, one launch (start us, length us, event | category | flops | bytes accessed | tf_op | source)
XLA Modules:
  0.0 208.6 jit_solution(5780138947608077798)
XLA Ops:
  4.9 10.2 %collective-permute-done.refs_1_.refs_2_ = bf16[27,32,256]{2,1,0:T(8,128)(2,1)S(1)} collective-permute-done((bf16[27,32,256]{2,1,0:T(8,128)(2,1)S(1)}, bf16[27,32,256]{2,1,0:T(8,128)(2,1)S(1)}, u32[]{:S(2)}, u32[]{:S(2)}) %collective-permute-start) | collective-permute-done | bytes 442400 | tf_op jit(solution)/shard_map/ppermute | solution.py:528
  20.1 4.4 %collective-permute-start.8 = (bf16[1,32,32,128]{3,2,1,0:T(8,128)(2,1)}, bf16[1,32,32,128]{3,2,1,0:T(8,128)(2,1)}, u32[]{:S(2)}, u32[]{:S(2)}) collective-permute-start(bf16[1,32,32,128]{3,2,1,0:T(8,128)(2,1)} %get-tuple-element.72), channel_id=1, source_target_pairs={{1,0},{2,1},{3,2},{4,3},{5,4},{6,5},{7,6},{8,7},{9,8},{10,9},{11,1... | collective-permute-start | bytes 786440 | tf_op jit(solution)/shard_map/ppermute | solution.py:537
  24.8 7.0 %collective-permute-done.4.refs_2_.refs_3_ = bf16[27,32,256]{2,1,0:T(8,128)(2,1)} collective-permute-done((bf16[27,32,256]{2,1,0:T(8,128)(2,1)S(1)}, bf16[27,32,256]{2,1,0:T(8,128)(2,1)}, u32[]{:S(2)}, u32[]{:S(2)}) %collective-permute-start.4) | collective-permute-done | bytes 442400 | tf_op jit(solution)/shard_map/ppermute | solution.py:534
  32.6 5.3 %collective-permute-start.3 = (bf16[1,32,32,128]{3,2,1,0:T(8,128)(2,1)S(1)}, bf16[1,32,32,128]{3,2,1,0:T(8,128)(2,1)S(1)}, u32[]{:S(2)}, u32[]{:S(2)}) collective-permute-start(bf16[1,32,32,128]{3,2,1,0:T(8,128)(2,1)S(1)} %get-tuple-element.74), channel_id=1, source_target_pairs={{1,0},{2,1},{3,2},{4,3},{5,4},{6,5},{7,6},{8,7},{9,8},{10,9},{11,1... | collective-permute-start | bytes 786440 | tf_op jit(solution)/shard_map/ppermute | solution.py:537
  37.9 6.3 %first_own.1.refs_5_ = f32[2,32,32,256]{3,2,1,0:T(8,128)S(1)} custom-call(bf16[1,32,32,128]{3,2,1,0:T(8,128)(2,1)S(1)} %collective-permute-done.7.refs_0_.low, bf16[2,32,32,128]{3,2,1,0:T(8,128)(2,1)S(1)} %copy-done, bf16[1,32,32,128]{3,2,1,0:T(8,128)(2,1)} %collective-permute-done.8.refs_2_.high, bf16[27,128,256]{2,1,0:T(8,128)(2,1)S(1)} %bitcast.10), custom_call_target="tpu_custom_call" | custom-call | flops 3623878656 | bytes 2818048 | tf_op jit(solution)/shard_map/first_own/pallas_call | solution.py:471
  44.2 4.4 %first_other.1.refs_6_ = f32[2,32,32,256]{3,2,1,0:T(8,128)S(1)} custom-call(bf16[2,32,32,128]{3,2,1,0:T(8,128)(2,1)S(1)} %collective-permute-done.1.refs_0_, bf16[27,32,256]{2,1,0:T(8,128)(2,1)S(1)} %collective-permute-done.refs_1_.refs_2_, bf16[27,32,256]{2,1,0:T(8,128)(2,1)} %collective-permute-done.4.refs_2_.refs_3_, ...), custom_call_target="tpu_custom_call" | custom-call | flops 2415919104 | bytes 4390912 | tf_op jit(solution)/shard_map/first_other/pallas_call | solution.py:471
  48.7 3.6 %first_rim.1 = (bf16[1,32,32,256]{3,2,1,0:T(8,128)(2,1)S(1)}, bf16[1,32,32,256]{3,2,1,0:T(8,128)(2,1)S(1)}) custom-call(bf16[1,32,32,128]{3,2,1,0:T(8,128)(2,1)S(1)} %collective-permute-done.2.refs_0_, bf16[1,32,32,128]{3,2,1,0:T(8,128)(2,1)S(1)} %collective-permute-done.3.refs_1_, bf16[27,32,256]{2,1,0:T(8,128)(2,1)S(1)} %collective-permute-done.refs_1_.refs_2_, ...), custom_call_target="tpu_custom_call" | custom-call | flops 1207959552 | bytes 4390912 | tf_op jit(solution)/shard_map/first_rim/pallas_call | solution.py:471
  54.5 5.2 %collective-permute-start.10 = (bf16[1,32,32,256]{3,2,1,0:T(8,128)(2,1)S(1)}, bf16[1,32,32,256]{3,2,1,0:T(8,128)(2,1)S(1)}, u32[]{:S(2)}, u32[]{:S(2)}) collective-permute-start(bf16[1,32,32,256]{3,2,1,0:T(8,128)(2,1)S(1)} %get-tuple-element.40.refs_0_.mid_0.refs_6_), channel_id=1, source_target_pairs={{1,0},{2,1},{3,2},{4,3},{5,4},{6,5},{7,6},{8,7},{9,8},{10,9},{11,1... | collective-permute-start | bytes 1572872 | tf_op jit(solution)/shard_map/ppermute | solution.py:537
  59.8 6.6 %second_local.1.refs_5_ = f32[2,32,32,256]{3,2,1,0:T(8,128)S(1)} custom-call(bf16[1,32,32,256]{3,2,1,0:T(8,128)(2,1)S(1)} %get-tuple-element.40.refs_0_.mid_0.refs_6_, bf16[1,32,32,256]{3,2,1,0:T(8,128)(2,1)S(1)} %get-tuple-element.39.refs_1_.mid_1.refs_7_, bf16[27,128,256]{2,1,0:T(8,128)(2,1)S(1)} %bitcast.5, ...), custom_call_target="tpu_custom_call" | custom-call | flops 4831838208 | bytes 4587520 | tf_op jit(solution)/shard_map/second_local/pallas_call | solution.py:471
  68.1 4.8 %second_rim.1 = (bf16[2,32,32,128]{3,2,1,0:T(8,128)(2,1)}, bf16[1,32,32,256]{3,2,1,0:T(8,128)(2,1)S(1)}, bf16[1,32,32,256]{3,2,1,0:T(8,128)(2,1)S(1)}) custom-call(bf16[1,32,32,256]{3,2,1,0:T(8,128)(2,1)S(1)} %collective-permute-done.9.refs_0_.low, bf16[1,32,32,256]{3,2,1,0:T(8,128)(2,1)S(1)} %collective-permute-done.10.refs_1_.high, ...), custom_call_target="tpu_custom_call" | custom-call | flops 2415919104 | bytes 7733248 | tf_op jit(solution)/shard_map/second_rim/pallas_call | solution.py:471
  73.0 6.2 %grad_two.1 = (f32[8,27,16,128]{3,2,1,0:T(8,128)S(1)}, bf16[8,27,16,128]{3,2,1,0:T(8,128)(2,1)S(1)}) custom-call(bf16[1,32,32,256]{3,2,1,0:T(8,128)(2,1)S(1)} %collective-permute-done.9.refs_0_.low, bf16[1,32,32,256]{3,2,1,0:T(8,128)(2,1)S(1)} %get-tuple-element.40.refs_0_.mid_0.refs_6_, ...), custom_call_target="tpu_custom_call" | custom-call | flops 3623878656 | bytes 8388608 | tf_op jit(solution)/shard_map/grad_two/pallas_call | solution.py:493
  79.2 3.2 %collective-permute-start.15 = (bf16[8,27,16,128]{3,2,1,0:T(8,128)(2,1)S(1)}, bf16[8,27,16,128]{3,2,1,0:T(8,128)(2,1)S(1)}, u32[]{:S(2)}, u32[]{:S(2)}) collective-permute-start(bf16[8,27,16,128]{3,2,1,0:T(8,128)(2,1)S(1)} %get-tuple-element.48), channel_id=1, source_target_pairs={{0,1},{1,0},{2,3},{3,2},{4,5},{5,4},{6,7},{7,6},{8,9},{9,8},{10,11... | collective-permute-start | bytes 2654216 | tf_op jit(solution)/shard_map/ppermute | solution.py:531
  82.4 4.4 %collective-permute-start.16 = (bf16[1,32,32,256]{3,2,1,0:T(8,128)(2,1)S(1)}, bf16[1,32,32,256]{3,2,1,0:T(8,128)(2,1)S(1)}, u32[]{:S(2)}, u32[]{:S(2)}) collective-permute-start(bf16[1,32,32,256]{3,2,1,0:T(8,128)(2,1)S(1)} %get-tuple-element.46.delta_0.refs_0_), channel_id=1, source_target_pairs={{1,0},{2,1},{3,2},{4,3},{5,4},{6,5},{7,6},{8,7},{9,8},{10,9},{11,1... | collective-permute-start | bytes 1572872 | tf_op jit(solution)/shard_map/ppermute | solution.py:537
  86.8 6.8 %back_local.1.refs_5_ = f32[2,32,32,256]{3,2,1,0:T(8,128)S(1)} custom-call(bf16[1,32,32,256]{3,2,1,0:T(8,128)(2,1)S(1)} %get-tuple-element.46.delta_0.refs_0_, bf16[1,32,32,256]{3,2,1,0:T(8,128)(2,1)S(1)} %get-tuple-element.45.delta_1.refs_1_, bf16[27,128,256]{2,1,0:T(8,128)(2,1)S(1)} %bitcast.7, bf16[27,64,256]{2,1,0:T(8,128)(2,1)S(1)} %collective-permute-done.11.refs_3_, ...), custom_call_target="tpu_custom_call" | custom-call | flops 4831838208 | bytes 4587520 | tf_op jit(solution)/shard_map/back_local/pallas_call | solution.py:471
  93.9 4.0 %back_rim.1 = (bf16[1,32,32,256]{3,2,1,0:T(8,128)(2,1)S(1)}, bf16[1,32,32,256]{3,2,1,0:T(8,128)(2,1)S(1)}) custom-call(bf16[1,32,32,256]{3,2,1,0:T(8,128)(2,1)S(1)} %collective-permute-done.14.refs_0_, bf16[1,32,32,256]{3,2,1,0:T(8,128)(2,1)S(1)} %collective-permute-done.16.refs_1_, bf16[27,128,256]{2,1,0:T(8,128)(2,1)S(1)} %bitcast.8, ...), custom_call_target="tpu_custom_call" | custom-call | flops 2415919104 | bytes 7733248 | tf_op jit(solution)/shard_map/back_rim/pallas_call | solution.py:471
  97.8 7.1 %grad_one.1 = (f32[8,27,16,128]{3,2,1,0:T(8,128)S(1)}, bf16[8,27,16,128]{3,2,1,0:T(8,128)(2,1)S(1)}) custom-call(bf16[1,32,32,128]{3,2,1,0:T(8,128)(2,1)S(1)} %collective-permute-done.7.refs_0_.low, bf16[2,32,32,128]{3,2,1,0:T(8,128)(2,1)S(1)} %copy-done, bf16[2,32,32,128]{3,2,1,0:T(8,128)(2,1)S(1)} %copy-done, ...), custom_call_target="tpu_custom_call" | custom-call | flops 3623878656 | bytes 8388608 | tf_op jit(solution)/shard_map/grad_one/pallas_call | solution.py:493
  107.8 12.1 %collective-permute-done.20.came = bf16[4,27,16,128]{3,2,1,0:T(8,128)(2,1)S(1)} collective-permute-done((bf16[4,27,16,128]{3,2,1,0:T(8,128)(2,1)S(1)}, bf16[4,27,16,128]{3,2,1,0:T(8,128)(2,1)S(1)}, u32[]{:S(2)}, u32[]{:S(2)}) %collective-permute-start.20) | collective-permute-done | bytes 442400 | tf_op jit(solution)/shard_map/ppermute | solution.py:534
  124.3 3.7 %collective-permute-done.22.rest_0_ = bf16[27,16,128]{2,1,0:T(8,128)(2,1)S(1)} collective-permute-done((bf16[27,16,128]{2,1,0:T(8,128)(2,1)S(1)}, bf16[27,16,128]{2,1,0:T(8,128)(2,1)S(1)}, u32[]{:S(2)}, u32[]{:S(2)}) %collective-permute-start.22) | collective-permute-done | bytes 110624 | tf_op jit(solution)/shard_map/ppermute | solution.py:425
  128.0 3.1 %collective-permute-done.23.rest_1_ = bf16[27,16,128]{2,1,0:T(8,128)(2,1)S(1)} collective-permute-done((bf16[27,16,128]{2,1,0:T(8,128)(2,1)S(1)}, bf16[27,16,128]{2,1,0:T(8,128)(2,1)S(1)}, u32[]{:S(2)}, u32[]{:S(2)}) %collective-permute-start.23) | collective-permute-done | bytes 110624 | tf_op jit(solution)/shard_map/ppermute | solution.py:425
  135.6 3.5 %collective-permute-done.28.rest_0_ = bf16[27,16,128]{2,1,0:T(8,128)(2,1)S(1)} collective-permute-done((bf16[27,16,128]{2,1,0:T(8,128)(2,1)S(1)}, bf16[27,16,128]{2,1,0:T(8,128)(2,1)S(1)}, u32[]{:S(2)}, u32[]{:S(2)}) %collective-permute-start.28) | collective-permute-done | bytes 110624 | tf_op jit(solution)/shard_map/ppermute | solution.py:425
  144.8 20.8 %collective-permute-done.32.came = bf16[4,27,16,128]{3,2,1,0:T(8,128)(2,1)S(1)} collective-permute-done((bf16[4,27,16,128]{3,2,1,0:T(8,128)(2,1)S(1)}, bf16[4,27,16,128]{3,2,1,0:T(8,128)(2,1)S(1)}, u32[]{:S(2)}, u32[]{:S(2)}) %collective-permute-start.32) | collective-permute-done | bytes 442400 | tf_op jit(solution)/shard_map/ppermute | solution.py:534
  165.7 5.6 %collective-permute-done.21.came = bf16[4,27,16,128]{3,2,1,0:T(8,128)(2,1)S(1)} collective-permute-done((bf16[4,27,16,128]{3,2,1,0:T(8,128)(2,1)S(1)}, bf16[4,27,16,128]{3,2,1,0:T(8,128)(2,1)S(1)}, u32[]{:S(2)}, u32[]{:S(2)}) %collective-permute-start.21) | collective-permute-done | bytes 442400 | tf_op jit(solution)/shard_map/ppermute | solution.py:534
  175.3 9.5 %first_back.1 = bf16[2,32,32,128]{3,2,1,0:T(8,128)(2,1)} custom-call(bf16[1,32,32,256]{3,2,1,0:T(8,128)(2,1)S(1)} %collective-permute-done.17.refs_0_, bf16[1,32,32,256]{3,2,1,0:T(8,128)(2,1)S(1)} %get-tuple-element.52.refs_1_.delta_0, bf16[1,32,32,256]{3,2,1,0:T(8,128)(2,1)S(1)} %get-tuple-element.51.refs_2_.delta_1, ...), custom_call_target="tpu_custom_call" | custom-call | flops 3623878656 | bytes 3866624 | tf_op jit(solution)/shard_map/first_back/pallas_call | solution.py:471
  198.3 5.6 %collective-permute-done.35.came = bf16[4,27,16,128]{3,2,1,0:T(8,128)(2,1)S(1)} collective-permute-done((bf16[4,27,16,128]{3,2,1,0:T(8,128)(2,1)S(1)}, bf16[4,27,16,128]{3,2,1,0:T(8,128)(2,1)S(1)}, u32[]{:S(2)}, u32[]{:S(2)}) %collective-permute-start.35) | collective-permute-done | bytes 442400 | tf_op jit(solution)/shard_map/ppermute | solution.py:534
  (86 shorter events, 54.2 us)
Async XLA Ops:
  1.9 13.2 %collective-permute-start = (bf16[27,32,256]{2,1,0:T(8,128)(2,1)S(1)}, bf16[27,32,256]{2,1,0:T(8,128)(2,1)S(1)}, u32[]{:S(2)}, u32[]{:S(2)}) collective-permute-start(bf16[27,32,256]{2,1,0:T(8,128)(2,1)S(1)} %constant_dynamic-slice_fusion.1), channel_id=1, source_target_pairs={{0,16},{16,0},{1,17},{17,1},{2,18},{18,2},{3,19},{19,3},{4,20},{20... | collective-permute-start | bytes 1327112 | tf_op jit(solution)/shard_map/ppermute | solution.py:528
  15.1 16.7 %collective-permute-start.1 = (bf16[2,32,32,128]{3,2,1,0:T(8,128)(2,1)}, bf16[2,32,32,128]{3,2,1,0:T(8,128)(2,1)S(1)}, u32[]{:S(2)}, u32[]{:S(2)}) collective-permute-start(bf16[2,32,32,128]{3,2,1,0:T(8,128)(2,1)} %mid_1.1), channel_id=1, source_target_pairs={{0,16},{16,0},{1,17},{17,1},{2,18},{18,2},{3,19},{19,3},{4,20},{20... | collective-permute-start | bytes 1572872 | tf_op jit(solution)/shard_map/ppermute | solution.py:528
  16.8 14.9 %collective-permute-start.4 = (bf16[27,32,256]{2,1,0:T(8,128)(2,1)S(1)}, bf16[27,32,256]{2,1,0:T(8,128)(2,1)}, u32[]{:S(2)}, u32[]{:S(2)}) collective-permute-start(bf16[27,32,256]{2,1,0:T(8,128)(2,1)S(1)} %collective-permute-done.refs_1_.refs_2_), channel_id=1, source_target_pairs={{0,2},{1,3},{2,0},{3,1},{4,6},{5,7},{6,4},{7,5},{8,10},{9,11},{10,... | collective-permute-start | bytes 1327112 | tf_op jit(solution)/shard_map/ppermute | solution.py:534
  20.1 12.1 %collective-permute-start.7 = (bf16[1,32,32,128]{3,2,1,0:T(8,128)(2,1)}, bf16[1,32,32,128]{3,2,1,0:T(8,128)(2,1)S(1)}, u32[]{:S(2)}, u32[]{:S(2)}) collective-permute-start(bf16[1,32,32,128]{3,2,1,0:T(8,128)(2,1)} %get-tuple-element.73), channel_id=1, source_target_pairs={{0,1},{1,2},{2,3},{3,4},{4,5},{5,6},{6,7},{7,8},{8,9},{9,10},{10,1... | collective-permute-start | bytes 786440 | tf_op jit(solution)/shard_map/ppermute | solution.py:537
  20.1 12.4 %collective-permute-start.8 = (bf16[1,32,32,128]{3,2,1,0:T(8,128)(2,1)}, bf16[1,32,32,128]{3,2,1,0:T(8,128)(2,1)}, u32[]{:S(2)}, u32[]{:S(2)}) collective-permute-start(bf16[1,32,32,128]{3,2,1,0:T(8,128)(2,1)} %get-tuple-element.72), channel_id=1, source_target_pairs={{1,0},{2,1},{3,2},{4,3},{5,4},{6,5},{7,6},{8,7},{9,8},{10,9},{11,1... | collective-permute-start | bytes 786440 | tf_op jit(solution)/shard_map/ppermute | solution.py:537
  24.7 19.5 %collective-permute-start.5 = (bf16[27,32,256]{2,1,0:T(8,128)(2,1)S(1)}, bf16[27,32,256]{2,1,0:T(8,128)(2,1)S(1)}, u32[]{:S(2)}, u32[]{:S(2)}) collective-permute-start(bf16[27,32,256]{2,1,0:T(8,128)(2,1)S(1)} %collective-permute-done.refs_1_.refs_2_), channel_id=1, source_target_pairs={{0,1},{1,0},{2,3},{3,2},{4,5},{5,4},{6,7},{7,6},{8,9},{9,8},{10,11... | collective-permute-start | bytes 1327112 | tf_op jit(solution)/shard_map/ppermute | solution.py:531
  31.7 12.5 %collective-permute-start.6 = (bf16[27,32,256]{2,1,0:T(8,128)(2,1)}, bf16[27,32,256]{2,1,0:T(8,128)(2,1)S(1)}, u32[]{:S(2)}, u32[]{:S(2)}) collective-permute-start(bf16[27,32,256]{2,1,0:T(8,128)(2,1)} %collective-permute-done.4.refs_2_.refs_3_), channel_id=1, source_target_pairs={{0,1},{1,0},{2,3},{3,2},{4,5},{5,4},{6,7},{7,6},{8,9},{9,8},{10,11... | collective-permute-start | bytes 1327112 | tf_op jit(solution)/shard_map/ppermute | solution.py:531
  31.7 22.1 %collective-permute-start.11 = (bf16[27,64,256]{2,1,0:T(8,128)(2,1)S(1)}, bf16[27,64,256]{2,1,0:T(8,128)(2,1)S(1)}, u32[]{:S(2)}, u32[]{:S(2)}) collective-permute-start(bf16[27,64,256]{2,1,0:T(8,128)(2,1)S(1)} %constant_dynamic-slice_fusion), channel_id=1, source_target_pairs={{0,16},{16,0},{1,17},{17,1},{2,18},{18,2},{3,19},{19,3},{4,20},{20... | collective-permute-start | bytes 2654216 | tf_op jit(solution)/shard_map/ppermute | solution.py:528
  32.3 16.4 %collective-permute-start.2 = (bf16[1,32,32,128]{3,2,1,0:T(8,128)(2,1)S(1)}, bf16[1,32,32,128]{3,2,1,0:T(8,128)(2,1)S(1)}, u32[]{:S(2)}, u32[]{:S(2)}) collective-permute-start(bf16[1,32,32,128]{3,2,1,0:T(8,128)(2,1)S(1)} %get-tuple-element.75), channel_id=1, source_target_pairs={{0,1},{1,2},{2,3},{3,4},{4,5},{5,6},{6,7},{7,8},{8,9},{9,10},{10,1... | collective-permute-start | bytes 786440 | tf_op jit(solution)/shard_map/ppermute | solution.py:537
  32.6 16.1 %collective-permute-start.3 = (bf16[1,32,32,128]{3,2,1,0:T(8,128)(2,1)S(1)}, bf16[1,32,32,128]{3,2,1,0:T(8,128)(2,1)S(1)}, u32[]{:S(2)}, u32[]{:S(2)}) collective-permute-start(bf16[1,32,32,128]{3,2,1,0:T(8,128)(2,1)S(1)} %get-tuple-element.74), channel_id=1, source_target_pairs={{1,0},{2,1},{3,2},{4,3},{5,4},{6,5},{7,6},{8,7},{9,8},{10,9},{11,1... | collective-permute-start | bytes 786440 | tf_op jit(solution)/shard_map/ppermute | solution.py:537
  53.8 14.3 %collective-permute-start.13 = (bf16[2,32,32,128]{3,2,1,0:T(8,128)(2,1)S(1)}, bf16[2,32,32,128]{3,2,1,0:T(8,128)(2,1)S(1)}, u32[]{:S(2)}, u32[]{:S(2)}) collective-permute-start(bf16[2,32,32,128]{3,2,1,0:T(8,128)(2,1)S(1)} %copy-done.3), channel_id=1, source_target_pairs={{0,16},{16,0},{1,17},{17,1},{2,18},{18,2},{3,19},{19,3},{4,20},{20... | collective-permute-start | bytes 1572872 | tf_op jit(solution)/shard_map/ppermute | solution.py:528
  54.3 13.8 %collective-permute-start.9 = (bf16[1,32,32,256]{3,2,1,0:T(8,128)(2,1)S(1)}, bf16[1,32,32,256]{3,2,1,0:T(8,128)(2,1)S(1)}, u32[]{:S(2)}, u32[]{:S(2)}) collective-permute-start(bf16[1,32,32,256]{3,2,1,0:T(8,128)(2,1)S(1)} %get-tuple-element.39.refs_1_.mid_1.refs_7_), channel_id=1, source_target_pairs={{0,1},{1,2},{2,3},{3,4},{4,5},{5,6},{6,7},{7,8},{8,9},{9,10},{10,1... | collective-permute-start | bytes 1572872 | tf_op jit(solution)/shard_map/ppermute | solution.py:537
  54.5 13.6 %collective-permute-start.10 = (bf16[1,32,32,256]{3,2,1,0:T(8,128)(2,1)S(1)}, bf16[1,32,32,256]{3,2,1,0:T(8,128)(2,1)S(1)}, u32[]{:S(2)}, u32[]{:S(2)}) collective-permute-start(bf16[1,32,32,256]{3,2,1,0:T(8,128)(2,1)S(1)} %get-tuple-element.40.refs_0_.mid_0.refs_6_), channel_id=1, source_target_pairs={{1,0},{2,1},{3,2},{4,3},{5,4},{6,5},{7,6},{8,7},{9,8},{10,9},{11,1... | collective-permute-start | bytes 1572872 | tf_op jit(solution)/shard_map/ppermute | solution.py:537
  79.2 14.4 %collective-permute-start.15 = (bf16[8,27,16,128]{3,2,1,0:T(8,128)(2,1)S(1)}, bf16[8,27,16,128]{3,2,1,0:T(8,128)(2,1)S(1)}, u32[]{:S(2)}, u32[]{:S(2)}) collective-permute-start(bf16[8,27,16,128]{3,2,1,0:T(8,128)(2,1)S(1)} %get-tuple-element.48), channel_id=1, source_target_pairs={{0,1},{1,0},{2,3},{3,2},{4,5},{5,4},{6,7},{7,6},{8,9},{9,8},{10,11... | collective-permute-start | bytes 2654216 | tf_op jit(solution)/shard_map/ppermute | solution.py:531
  104.9 39.5 %collective-permute-start.19 = (bf16[8,27,16,128]{3,2,1,0:T(8,128)(2,1)S(1)}, bf16[8,27,16,128]{3,2,1,0:T(8,128)(2,1)S(1)}, u32[]{:S(2)}, u32[]{:S(2)}) collective-permute-start(bf16[8,27,16,128]{3,2,1,0:T(8,128)(2,1)S(1)} %get-tuple-element.54), channel_id=1, source_target_pairs={{0,1},{1,0},{2,3},{3,2},{4,5},{5,4},{6,7},{7,6},{8,9},{9,8},{10,11... | collective-permute-start | bytes 2654216 | tf_op jit(solution)/shard_map/ppermute | solution.py:531
  107.8 12.2 %collective-permute-start.20 = (bf16[4,27,16,128]{3,2,1,0:T(8,128)(2,1)S(1)}, bf16[4,27,16,128]{3,2,1,0:T(8,128)(2,1)S(1)}, u32[]{:S(2)}, u32[]{:S(2)}) collective-permute-start(bf16[4,27,16,128]{3,2,1,0:T(8,128)(2,1)S(1)} %get-tuple-element.55), channel_id=1, source_target_pairs={{0,2},{1,3},{2,0},{3,1},{4,6},{5,7},{6,4},{7,5},{8,10},{9,11},{10,... | collective-permute-start | bytes 1327112 | tf_op jit(solution)/shard_map/ppermute | solution.py:534
  135.6 37.1 %collective-permute-start.17 = (bf16[1,32,32,256]{3,2,1,0:T(8,128)(2,1)S(1)}, bf16[1,32,32,256]{3,2,1,0:T(8,128)(2,1)S(1)}, u32[]{:S(2)}, u32[]{:S(2)}) collective-permute-start(bf16[1,32,32,256]{3,2,1,0:T(8,128)(2,1)S(1)} %get-tuple-element.51.refs_2_.delta_1), channel_id=1, source_target_pairs={{0,1},{1,2},{2,3},{3,4},{4,5},{5,6},{6,7},{7,8},{8,9},{9,10},{10,1... | collective-permute-start | bytes 1572872 | tf_op jit(solution)/shard_map/ppermute | solution.py:537
  139.1 36.2 %collective-permute-start.18 = (bf16[1,32,32,256]{3,2,1,0:T(8,128)(2,1)S(1)}, bf16[1,32,32,256]{3,2,1,0:T(8,128)(2,1)S(1)}, u32[]{:S(2)}, u32[]{:S(2)}) collective-permute-start(bf16[1,32,32,256]{3,2,1,0:T(8,128)(2,1)S(1)} %get-tuple-element.52.refs_1_.delta_0), channel_id=1, source_target_pairs={{1,0},{2,1},{3,2},{4,3},{5,4},{6,5},{7,6},{8,7},{9,8},{10,9},{11,1... | collective-permute-start | bytes 1572872 | tf_op jit(solution)/shard_map/ppermute | solution.py:537
  142.1 23.4 %collective-permute-start.32 = (bf16[4,27,16,128]{3,2,1,0:T(8,128)(2,1)S(1)}, bf16[4,27,16,128]{3,2,1,0:T(8,128)(2,1)S(1)}, u32[]{:S(2)}, u32[]{:S(2)}) collective-permute-start(bf16[4,27,16,128]{3,2,1,0:T(8,128)(2,1)S(1)} %sum_two_levels.1.own), channel_id=1, source_target_pairs={{0,2},{1,3},{2,0},{3,1},{4,6},{5,7},{6,4},{7,5},{8,10},{9,11},{10,... | collective-permute-start | bytes 1327112 | tf_op jit(solution)/shard_map/ppermute | solution.py:534
  144.7 26.7 %collective-permute-start.21 = (bf16[4,27,16,128]{3,2,1,0:T(8,128)(2,1)S(1)}, bf16[4,27,16,128]{3,2,1,0:T(8,128)(2,1)S(1)}, u32[]{:S(2)}, u32[]{:S(2)}) collective-permute-start(bf16[4,27,16,128]{3,2,1,0:T(8,128)(2,1)S(1)} %get-tuple-element.59), channel_id=1, source_target_pairs={{0,2},{1,3},{2,0},{3,1},{4,6},{5,7},{6,4},{7,5},{8,10},{9,11},{10,... | collective-permute-start | bytes 1327112 | tf_op jit(solution)/shard_map/ppermute | solution.py:534
  165.6 30.5 %collective-permute-start.36 = (bf16[8,27,16,128]{3,2,1,0:T(8,128)(2,1)S(1)}, bf16[8,27,16,128]{3,2,1,0:T(8,128)(2,1)S(1)}, u32[]{:S(2)}, u32[]{:S(2)}) collective-permute-start(bf16[8,27,16,128]{3,2,1,0:T(8,128)(2,1)S(1)} %sum_two_sides.1.own), channel_id=1, source_target_pairs={{0,1},{1,0},{2,3},{3,2},{4,5},{5,4},{6,7},{7,6},{8,9},{9,8},{10,11... | collective-permute-start | bytes 2654216 | tf_op jit(solution)/shard_map/ppermute | solution.py:531
  171.4 13.4 %collective-permute-start.25 = (bf16[27,16,128]{2,1,0:T(8,128)(2,1)S(1)}, bf16[27,16,128]{2,1,0:T(8,128)(2,1)S(1)}, u32[]{:S(2)}, u32[]{:S(2)}) collective-permute-start(bf16[27,16,128]{2,1,0:T(8,128)(2,1)S(1)} %get-tuple-element.66), channel_id=1, source_target_pairs={{0,4},{1,5},{2,6},{3,7},{4,8},{5,9},{6,10},{7,11},{8,12},{9,13},{1... | collective-permute-start | bytes 331784 | tf_op jit(solution)/shard_map/ppermute | solution.py:425
  172.5 12.2 %collective-permute-start.26 = (bf16[27,16,128]{2,1,0:T(8,128)(2,1)S(1)}, bf16[27,16,128]{2,1,0:T(8,128)(2,1)S(1)}, u32[]{:S(2)}, u32[]{:S(2)}) collective-permute-start(bf16[27,16,128]{2,1,0:T(8,128)(2,1)S(1)} %get-tuple-element.67), channel_id=1, source_target_pairs={{0,8},{1,9},{2,10},{3,11},{4,12},{5,13},{6,14},{7,15},{8,0},{9,1},... | collective-permute-start | bytes 331784 | tf_op jit(solution)/shard_map/ppermute | solution.py:425
  172.7 12.1 %collective-permute-start.27 = (bf16[27,16,128]{2,1,0:T(8,128)(2,1)S(1)}, bf16[27,16,128]{2,1,0:T(8,128)(2,1)S(1)}, u32[]{:S(2)}, u32[]{:S(2)}) collective-permute-start(bf16[27,16,128]{2,1,0:T(8,128)(2,1)S(1)} %get-tuple-element.68), channel_id=1, source_target_pairs={{0,12},{1,13},{2,14},{3,15},{4,0},{5,1},{6,2},{7,3},{8,4},{9,5},{1... | collective-permute-start | bytes 331784 | tf_op jit(solution)/shard_map/ppermute | solution.py:425
  (18 other events, 195.1 us)
